TPU v7x, 128 devices: a whole 4x4x4 slice. The times are simulated.
128 devices in a mesh: gx: 4 (over z), gy: 32 (over x, y, core).
Axes of the slice: x: 4, y: 4, z: 4, core: 2. Of those that a mesh axis runs over, the one named last changes fastest.
Arguments:
- gauss_params: float32 [55, 262144], P(None, ('gx', 'gy')), may hold values from -16 to 2064, as said below
- first_moment: float32 [55, 262144], P(None, ('gx', 'gy')), may hold values from -0.3 to 0.3
- second_moment: float32 [55, 262144], P(None, ('gx', 'gy')), may hold values from 0.001 to 0.1
- splat_lists: int32 [2, 2048, 512], P(None, ('gx', 'gy')), may hold values from 0 to 262143, as said below
- tile_ids: int32 [2, 2048], P(None, ('gx', 'gy')), may hold values from 0 to 2047, as said below
- targets: float32 [2, 2048, 3, 256], P(None, ('gx', 'gy')), may hold values from 0 to 1
- camera: float32 [2, 2], replicated, may hold values from -3 to 3
Outputs:
- updated_params: float32 [55, 262144], P(None, ('gx', 'gy'))
- updated_first: float32 [55, 262144], P(None, ('gx', 'gy'))
- updated_second: float32 [55, 262144], P(None, ('gx', 'gy'))
- rendered: float32 [2, 2048, 3, 256], P(None, ('gx', 'gy'))
- loss: float32 [2], replicated
Inputs may be any that keep to these rules, and one draw needn't show every extreme that they name: `gauss_params`: rows of each column: x and y (positions scaled by depth), depth z in [1, 2], two log scales, an angle, an opacity logit, then 16 harmonic coefficients for red, green and blue in turn. `splat_lists`: gaussian ids; the Gaussians with ids k * 2048 to (k + 1) * 2048 - 1 belong to device k along gx+gy. In each step, the entries of one device's 16 tile slots name Gaussians of one owner at most 128 times, and some owner is named exactly 128 times by every device. `tile_ids`: image tiles numbered row by row over 64 columns; within a step, slots show distinct tiles while 2048 <= 2048.
All inputs are finite; a program needn't handle non-finite values.
Results may differ from a plain program's by a relative error of at most 0.0014.
Values sent between devices are 32-bit elements; how exact they have to be, the bound alone decides.
A program may use at most 64 MiB of HBM per device.

v0:
```python
import jax
import jax.numpy as jnp
from jax import lax
from jax.sharding import PartitionSpec as P

SIDE = 16
NCOEF = 16
STEPS = 2
IMG_TX = 64
IMG_TY = 32


beta_one = 0.9
beta_two = 0.999
adam_eps = 1e-08
learn_rate = 0.01
adam_start = 1000
band_zero = 0.28209479177387814
band_one = 0.4886025119029199
band_two = (
    1.0925484305920792,
    -1.0925484305920792,
    0.31539156525252005,
    -1.0925484305920792,
    0.5462742152960396,
)
band_three = (
    -0.5900435899266435,
    2.890611442640554,
    -0.4570457994644658,
    0.3731763325901154,
    -0.4570457994644658,
    1.445305721320277,
    -0.5900435899266435,
)


def harmonics(ray_x, ray_y, ray_z):
    sq_x = ray_x * ray_x
    sq_y = ray_y * ray_y
    sq_z = ray_z * ray_z
    return jnp.stack(
        [
            band_zero * jnp.ones_like(ray_x),
            -band_one * ray_y,
            band_one * ray_z,
            -band_one * ray_x,
            band_two[0] * ray_x * ray_y,
            band_two[1] * ray_y * ray_z,
            band_two[2] * (2.0 * sq_z - sq_x - sq_y),
            band_two[3] * ray_x * ray_z,
            band_two[4] * (sq_x - sq_y),
            band_three[0] * ray_y * (3.0 * sq_x - sq_y),
            band_three[1] * ray_x * ray_y * ray_z,
            band_three[2] * ray_y * (4.0 * sq_z - sq_x - sq_y),
            band_three[3] * ray_z * (2.0 * sq_z - 3.0 * sq_x - 3.0 * sq_y),
            band_three[4] * ray_x * (4.0 * sq_z - sq_x - sq_y),
            band_three[5] * ray_z * (sq_x - sq_y),
            band_three[6] * ray_x * (sq_x - 3.0 * sq_y),
        ]
    )


def project(gauss_rows, camera_row):
    image_width = 1.0 * SIDE * IMG_TX
    image_height = 1.0 * SIDE * IMG_TY
    depth_z = gauss_rows[2]
    screen_u = (gauss_rows[0] - camera_row[0]) / depth_z
    screen_v = (gauss_rows[1] - camera_row[1]) / depth_z
    inv_one = depth_z * depth_z * jnp.exp(-2.0 * gauss_rows[3])
    inv_two = depth_z * depth_z * jnp.exp(-2.0 * gauss_rows[4])
    cosine = jnp.cos(gauss_rows[5])
    sine_angle = jnp.sin(gauss_rows[5])
    conic_a = cosine * cosine * inv_one + sine_angle * sine_angle * inv_two
    conic_b = cosine * sine_angle * (inv_one - inv_two)
    conic_c = sine_angle * sine_angle * inv_one + cosine * cosine * inv_two
    opacity = 0.99 * jax.nn.sigmoid(gauss_rows[6])
    ray_x = (screen_u - 0.5 * image_width) / image_width
    ray_y = (screen_v - 0.5 * image_height) / image_width
    factor = lax.rsqrt(ray_x * ray_x + ray_y * ray_y + 1.0)
    harmonic_basis = harmonics(ray_x * factor, ray_y * factor, factor)
    coeffs = gauss_rows[7:].reshape(3, NCOEF, gauss_rows.shape[1])
    colour = 0.5 + jnp.sum(coeffs * harmonic_basis[None], axis=1)
    geometry = jnp.stack([screen_u, screen_v, conic_a, conic_b, conic_c, opacity])
    return jnp.concatenate([geometry, colour], 0)


def pixel_grid(tile_row):
    cell_index = jnp.arange(SIDE * SIDE, dtype=jnp.int32)
    column = (tile_row % IMG_TX)[:, None] * SIDE + cell_index % SIDE
    row_pix = (tile_row // IMG_TX)[:, None] * SIDE + cell_index // SIDE
    return jnp.stack([column, row_pix], 1).astype(jnp.float32) + 0.5


def lower_mask(dtype):
    return (
        lax.broadcasted_iota(jnp.int32, (128, 128), 0)
        > lax.broadcasted_iota(jnp.int32, (128, 128), 1)
    ).astype(dtype)


def prefix_sum(log_keep):
    block_count = log_keep.shape[0] // 128
    blocks = log_keep.reshape(block_count, 128, log_keep.shape[1])
    within = jnp.einsum(
        "ij,bjp->bip", lower_mask(jnp.float32), blocks, precision=lax.Precision.HIGHEST
    )
    totals = jnp.sum(blocks, axis=1)
    carry_in = jnp.cumsum(totals, axis=0) - totals
    return (within + carry_in[:, None, :]).reshape(log_keep.shape)


def render(splat_rows, centres):
    delta_x = centres[0][None, :] - splat_rows[0][:, None]
    delta_y = centres[1][None, :] - splat_rows[1][:, None]
    exponent = -0.5 * (
        splat_rows[2][:, None] * delta_x * delta_x
        + 2.0 * splat_rows[3][:, None] * delta_x * delta_y
        + splat_rows[4][:, None] * delta_y * delta_y
    )
    opaque = splat_rows[5][:, None] * jnp.exp(exponent)
    log_keep = jnp.log1p(-opaque)
    weight = jnp.exp(prefix_sum(log_keep)) * opaque
    return jnp.dot(
        splat_rows[6:9], weight, precision=lax.Precision.HIGHEST, preferred_element_type=jnp.float32
    )


def raw_terms(gauss_rows, centres, target, camera_row):
    picture, pullback = jax.vjp(
        lambda values: render(project(values, camera_row), centres), gauss_rows
    )
    residual = picture - target
    return (picture, pullback(residual)[0], 0.5 * jnp.sum(residual * residual))


def bucket_positions(owner_of, owners, capacity):
    slot_count = owner_of.shape[0]
    block_count = slot_count // 128
    member = (owner_of[:, None] == jnp.arange(owners, dtype=jnp.int32)[None, :]).reshape(
        block_count, 128, owners
    )
    blocks = member.astype(jnp.bfloat16)
    within = jnp.einsum(
        "ij,bjo->bio", lower_mask(jnp.bfloat16), blocks, preferred_element_type=jnp.float32
    )
    totals = within[:, 127, :] + blocks[:, 127, :].astype(jnp.float32)
    carry_in = jnp.cumsum(totals, axis=0) - totals
    ahead_of = within + carry_in[:, None, :]
    rank_in = jnp.sum(jnp.where(member, ahead_of, 0.0), axis=2).reshape(slot_count)
    return owner_of * capacity + rank_in.astype(jnp.int32)


def route_ids(request):
    return lax.all_to_all(request, ("gx", "gy"), split_axis=0, concat_axis=0, tiled=True)


def route_rows(outgoing):
    return lax.all_to_all(outgoing, ("gx", "gy"), split_axis=1, concat_axis=1, tiled=True)


def adam_update(params, moment_one, second, gradient, step_index):
    step_count = adam_start + step_index + 1
    moment_one = beta_one * moment_one + (1.0 - beta_one) * gradient
    second = beta_two * second + (1.0 - beta_two) * gradient * gradient
    scaled_first = moment_one / (1.0 - beta_one**step_count)
    scaled_second = second / (1.0 - beta_two**step_count)
    params = params - learn_rate * scaled_first / (jnp.sqrt(scaled_second) + adam_eps)
    return (params, moment_one, second)


def per_device(gauss_params, first_moment, second_moment, splat_lists, tile_ids, targets, camera):
    owners = lax.axis_size(("gx", "gy"))
    local_count = gauss_params.shape[1]
    tile_count = splat_lists.shape[1]
    list_length = splat_lists.shape[2]
    capacity = 2 * tile_count * list_length // owners
    params, moment_one, moment_two = (gauss_params, first_moment, second_moment)
    pictures = []
    local_losses = []
    for step_index in range(STEPS):
        camera_row = camera[step_index]
        listed = splat_lists[step_index].reshape(-1)
        owner_of = listed // local_count
        local_id = listed % local_count
        slot_pos = bucket_positions(owner_of, owners, capacity)
        request = jnp.zeros((owners * capacity,), jnp.int32).at[slot_pos].set(local_id)
        wanted = route_ids(request)
        centres = pixel_grid(tile_ids[step_index])
        reply = route_rows(params[:, wanted])
        gathered = jnp.moveaxis(
            reply[:, slot_pos].reshape(params.shape[0], tile_count, list_length), 1, 0
        )
        picture, slot_grads, halves = lax.map(
            lambda tile_parts: raw_terms(tile_parts[0], tile_parts[1], tile_parts[2], camera_row),
            (gathered, centres, targets[step_index]),
        )
        field_count = slot_grads.shape[1]
        flat_grads = jnp.moveaxis(slot_grads, 0, 1).reshape(field_count, tile_count * list_length)
        outgoing = (
            jnp.zeros((field_count, owners * capacity), jnp.float32).at[:, slot_pos].set(flat_grads)
        )
        incoming = route_rows(outgoing)
        summed = jnp.zeros((field_count, local_count), jnp.float32).at[:, wanted].add(incoming)
        params, moment_one, moment_two = adam_update(
            params, moment_one, moment_two, summed, step_index
        )
        pictures.append(picture)
        local_losses.append(jnp.sum(halves))
    totals = lax.psum(jnp.stack(local_losses), ("gx", "gy"))
    loss_values = totals / (3.0 * SIDE * SIDE * tile_count * owners)
    return (params, moment_one, moment_two, jnp.stack(pictures), loss_values)


def solution(mesh):
    in_specs = (
        P(None, ("gx", "gy")),
        P(None, ("gx", "gy")),
        P(None, ("gx", "gy")),
        P(None, ("gx", "gy"), None),
        P(None, ("gx", "gy")),
        P(None, ("gx", "gy"), None, None),
        P(),
    )
    out_specs = (
        P(None, ("gx", "gy")),
        P(None, ("gx", "gy")),
        P(None, ("gx", "gy")),
        P(None, ("gx", "gy"), None, None),
        P(),
    )
    return jax.shard_map(
        per_device, mesh=mesh, in_specs=in_specs, out_specs=out_specs, check_vma=False
    )
```

profile of v0, /device:TPU:1, one launch (start us, length us, event | category | flops | bytes accessed | tf_op | source)
XLA Modules:
  0.0 1398.2 jit_solution(10457255492031290287)
XLA Ops:
  4.4 2.6 select_reduce_fusion.1
  7.2 31.0 %scatter_custom_fusion = s32[16384]{0:T(1024)} fusion(s32[8192]{0:T(1024)S(1)} %bitcast.939, s32[8192]{0:T(1024)S(1)} %add_select_fusion.2, s32[]{:T(128)} %constant.452.clone.1), kind=kCustom, calls=%fused_computation.507 | custom fusion | bytes 65540 | tf_op jit(solution)/shard_map/scatter | solution.py:187
  38.3 11.5 all-to-all-start
  52.7 2.6 select_reduce_fusion
  55.8 3.5 all-to-all-done
  59.4 54.4 %gather_fusion = f32[16384,55]{1,0:T(8,128)} fusion(f32[55,2048]{0,1:T(8,128)S(1)} %copy.115, s32[16384]{0:T(1024)S(1)} %broadcast_clamp_fusion.1), kind=kCustom, calls=%fused_computation | custom fusion | bytes 7274496 | tf_op jit(solution)/shard_map/gather | solution.py:190
  113.8 6.8 copy.116
  120.6 6.6 all-to-all-start.1
  127.4 31.0 %scatter_custom_fusion.3 = s32[16384]{0:T(1024)} fusion(s32[8192]{0:T(1024)S(1)} %bitcast.936, s32[8192]{0:T(1024)S(1)} %add_select_fusion, s32[]{:T(128)} %constant.452.clone.1), kind=kCustom, calls=%fused_computation.505 | custom fusion | bytes 65540 | tf_op jit(solution)/shard_map/scatter | solution.py:187
  159.5 14.9 %all-to-all-done.1 = f32[55,128,128]{2,0,1:T(8,128)} async-done(((f32[55,128,128]{2,0,1:T(8,128)}), f32[55,128,128]{2,0,1:T(8,128)}, u32[]{:S(2)}, u32[]{:S(2)}) %all-to-all-start.1) | async-done | bytes 3604512 | tf_op jit(solution)/shard_map/all_to_all | solution.py:159
  174.5 4.5 all-to-all-start.3
  179.0 6.8 copy.117
  185.8 31.1 %gather_fusion.1 = f32[8192,55]{1,0:T(8,128)} fusion(f32[55,16384]{0,1:T(8,128)} %bitcast.744, s32[8192]{0:T(1024)S(1)} %broadcast_clamp_fusion.3), kind=kCustom, calls=%fused_computation.1 | custom fusion | bytes 3637248 | tf_op jit(solution)/shard_map/gather | solution.py:192
  216.9 3.8 copy.118
  222.2 269.3 %while.32 = (s32[]{:T(128)}, f32[16,3,256]{2,0,1:T(8,128)S(1)}, f32[16,55,512]{2,1,0:T(8,128)}, f32[16]{0:T(128)S(1)}, f32[16,55,512]{2,1,0:T(8,128)}, /*index=5...) while((s32[]{:T(128)}, f32[16,3,256]{2,0,1:T(8,128)S(1)}, ...), condition=%wide.region_17.18_spmd, body=%wide.region_3.17_spmd.sunk | while | flops 431942400 | bytes 11435933 | solution.py:194
  242.9 2.3 broadcast_multiply_fusion.21
  276.5 2.3 broadcast_multiply_fusion.21
  293.3 2.3 broadcast_multiply_fusion.21
  343.8 2.3 broadcast_multiply_fusion.21
  491.5 2.5 copy.120
  495.4 2.8 copy.121
  498.1 24.7 %scatter_custom_fusion.1 = f32[55,16384]{0,1:T(8,128)} fusion(s32[8192]{0:T(1024)S(1)} %bitcast.941, f32[8192,55]{1,0:T(8,128)} %copy.121, f32[]{:T(128)} %constant.451.clone.1), kind=kCustom, calls=%fused_computation.430 | custom fusion | bytes 3604992 | tf_op jit(solution)/shard_map/scatter | solution.py:201
  522.9 6.7 copy.122
  529.6 10.3 all-to-all-start.2
  540.1 47.2 %all-to-all-done.2 = f32[55,128,128]{2,0,1:T(8,128)} async-done(((f32[55,128,128]{2,0,1:T(8,128)}), f32[55,128,128]{2,0,1:T(8,128)}, u32[]{:S(2)}, u32[]{:S(2)}) %all-to-all-start.2) | async-done | bytes 3604512 | tf_op jit(solution)/shard_map/all_to_all | solution.py:159
  587.2 2.7 copy.123
  590.4 3.9 copy.162
  594.4 6.9 copy.124
  601.3 98.5 %scatter_custom_fusion.2 = f32[55,2048]{0,1:T(8,128)S(1)} fusion(s32[16384]{0:T(1024)S(1)} %bitcast.929, f32[16384,55]{1,0:T(8,128)} %copy.124, f32[]{:T(128)} %constant.451.clone.1), kind=kCustom, calls=%fused_computation.446 | custom fusion | flops 901120 | bytes 451072 | tf_op jit(solution)/shard_map/scatter-add | solution.py:204
  701.8 54.4 %gather_fusion.2 = f32[16384,55]{1,0:T(8,128)} fusion(f32[55,2048]{0,1:T(8,128)S(1)} %copy.128, s32[16384]{0:T(1024)S(1)} %broadcast_clamp_fusion), kind=kCustom, calls=%fused_computation.2 | custom fusion | bytes 7274496 | tf_op jit(solution)/shard_map/gather | solution.py:190
  756.2 6.8 copy.129
  763.0 5.9 all-to-all-start.4
  768.9 47.2 %all-to-all-done.4 = f32[55,128,128]{2,0,1:T(8,128)} async-done(((f32[55,128,128]{2,0,1:T(8,128)}), f32[55,128,128]{2,0,1:T(8,128)}, u32[]{:S(2)}, u32[]{:S(2)}) %all-to-all-start.4) | async-done | bytes 3604512 | tf_op jit(solution)/shard_map/all_to_all | solution.py:159
  816.1 6.8 copy.130
  822.9 31.1 %gather_fusion.3 = f32[8192,55]{1,0:T(8,128)} fusion(f32[55,16384]{0,1:T(8,128)} %bitcast.745, s32[8192]{0:T(1024)S(1)} %broadcast_clamp_fusion.2), kind=kCustom, calls=%fused_computation.3 | custom fusion | bytes 3637248 | tf_op jit(solution)/shard_map/gather | solution.py:192
  854.0 3.8 copy.131
  859.3 280.4 %while.33 = (s32[]{:T(128)}, f32[16,3,256]{2,0,1:T(8,128)S(1)}, f32[16,55,512]{2,1,0:T(8,128)}, f32[16]{0:T(128)S(1)}, f32[16,55,512]{2,1,0:T(8,128)}, /*index=5...) while((s32[]{:T(128)}, f32[16,3,256]{2,0,1:T(8,128)S(1)}, ...), condition=%wide.region_37.38_spmd, body=%wide.region_23.37_spmd.sunk | while | flops 431942400 | bytes 11435933 | solution.py:194
  1139.8 2.5 copy.133
  1143.6 2.8 copy.134
  1146.4 24.7 %scatter_custom_fusion.4 = f32[55,16384]{0,1:T(8,128)} fusion(s32[8192]{0:T(1024)S(1)} %bitcast.938, f32[8192,55]{1,0:T(8,128)} %copy.134, f32[]{:T(128)} %constant.451.clone.1), kind=kCustom, calls=%fused_computation.428 | custom fusion | bytes 3604992 | tf_op jit(solution)/shard_map/scatter | solution.py:201
  1171.1 6.7 copy.135
  1177.8 5.3 all-to-all-start.5
  1185.7 96.0 %psum.7 = f32[2]{0:T(128)S(1)} all-reduce(f32[2]{0:T(128)S(1)} %pad_maximum_fusion.1), channel_id=1, replica_groups=mesh['gx'=4,'gy'=32] {'gx','gy'}, use_global_device_ids=true, to_apply=%region_42.43 | all-reduce | flops 2 | bytes 16 | tf_op jit(solution)/shard_map/psum | solution.py:210
  1282.9 2.7 copy.136
  1286.1 3.9 copy.166
  1290.1 6.9 copy.137
  1297.0 98.3 %scatter_custom_fusion.5 = f32[55,2048]{0,1:T(8,128)S(1)} fusion(s32[16384]{0:T(1024)S(1)} %bitcast.931, f32[16384,55]{1,0:T(8,128)} %copy.137, f32[]{:T(128)} %constant.451.clone.1), kind=kCustom, calls=%fused_computation.444 | custom fusion | flops 901120 | bytes 451072 | tf_op jit(solution)/shard_map/scatter-add | solution.py:204
  1395.6 2.4 divide_subtract_fusion
  (1323 shorter events, 538.4 us)
Async XLA Ops:
  38.3 21.0 %all-to-all-start = ((s32[128,128,1]{1,2,0:T(1,128)}), s32[128,128,1]{1,2,0:T(1,128)S(1)}, u32[]{:S(2)}, u32[]{:S(2)}) async-start(s32[128,128,1]{1,2,0:T(1,128)} %bitcast.100), calls=%async_computation | async-start | bytes 131072 | tf_op jit(solution)/shard_map/all_to_all | solution.py:155
  49.8 5.5 copy-start.5
  120.5 37.9 %copy-start.7 = (s32[2,16]{1,0:T(2,128)S(1)}, s32[2,16]{1,0:T(2,128)}, u32[]{:S(2)}) copy-start(s32[2,16]{1,0:T(2,128)} %param.15) | copy-start | bytes 388
  120.5 38.2 %copy-start.8 = (f32[2,2]{1,0:T(2,128)S(1)}, f32[2,2]{1,0:T(2,128)}, u32[]{:S(2)}) copy-start(f32[2,2]{1,0:T(2,128)} %param.17) | copy-start | bytes 52
  120.5 38.3 %copy-start.6 = (f32[2,16,3,256]{3,1,2,0:T(8,128)S(1)}, f32[2,16,3,256]{3,1,2,0:T(8,128)}, u32[]{:S(2)}) copy-start(f32[2,16,3,256]{3,1,2,0:T(8,128)} %param.16) | copy-start | bytes 294916
  120.6 53.9 %all-to-all-start.1 = ((f32[55,128,128]{2,0,1:T(8,128)}), f32[55,128,128]{2,0,1:T(8,128)}, u32[]{:S(2)}, u32[]{:S(2)}) async-start(f32[55,128,128]{2,0,1:T(8,128)} %copy.116), calls=%async_computation.1 | async-start | bytes 7340032 | tf_op jit(solution)/shard_map/all_to_all | solution.py:159
  174.5 355.2 %all-to-all-start.3 = ((s32[128,128,1]{1,2,0:T(1,128)}), s32[128,128,1]{1,2,0:T(1,128)S(1)}, u32[]{:S(2)}, u32[]{:S(2)}) async-start(s32[128,128,1]{1,2,0:T(1,128)} %bitcast.120), calls=%async_computation.3 | async-start | bytes 131072 | tf_op jit(solution)/shard_map/all_to_all | solution.py:155
  529.6 57.6 %all-to-all-start.2 = ((f32[55,128,128]{2,0,1:T(8,128)}), f32[55,128,128]{2,0,1:T(8,128)}, u32[]{:S(2)}, u32[]{:S(2)}) async-start(f32[55,128,128]{2,0,1:T(8,128)} %copy.122), calls=%async_computation.2 | async-start | bytes 7340032 | tf_op jit(solution)/shard_map/all_to_all | solution.py:159
  594.3 105.8 %copy-start.2 = (f32[55,2048]{1,0:T(8,128)S(1)}, f32[55,2048]{1,0:T(8,128)}, u32[]{:S(2)}) copy-start(f32[55,2048]{1,0:T(8,128)} %param.12) | copy-start | bytes 1351684
  594.3 105.8 %copy-start.4 = (f32[55,2048]{1,0:T(8,128)S(1)}, f32[55,2048]{1,0:T(8,128)}, u32[]{:S(2)}) copy-start(f32[55,2048]{1,0:T(8,128)} %param.13) | copy-start | bytes 1351684
  701.5 54.8 %copy-start = (f32[55,2048]{1,0:T(8,128)}, f32[55,2048]{1,0:T(8,128)S(1)}, u32[]{:S(2)}) copy-start(f32[55,2048]{1,0:T(8,128)S(1)} %divide_subtract_fusion.1) | copy-start | bytes 1351684
  763.0 53.1 %all-to-all-start.4 = ((f32[55,128,128]{2,0,1:T(8,128)}), f32[55,128,128]{2,0,1:T(8,128)}, u32[]{:S(2)}, u32[]{:S(2)}) async-start(f32[55,128,128]{2,0,1:T(8,128)} %copy.129), calls=%async_computation.4 | async-start | bytes 7340032 | tf_op jit(solution)/shard_map/all_to_all | solution.py:159
  1177.8 105.1 %all-to-all-start.5 = ((f32[55,128,128]{2,0,1:T(8,128)}), f32[55,128,128]{2,0,1:T(8,128)}, u32[]{:S(2)}, u32[]{:S(2)}) async-start(f32[55,128,128]{2,0,1:T(8,128)} %copy.135), calls=%async_computation.5 | async-start | bytes 7340032 | tf_op jit(solution)/shard_map/all_to_all | solution.py:159
  1290.1 105.6 %copy-start.1 = (f32[55,2048]{1,0:T(8,128)S(1)}, f32[55,2048]{1,0:T(8,128)}, u32[]{:S(2)}) copy-start(f32[55,2048]{1,0:T(8,128)} %copy-done) | copy-start | bytes 1351684
  1290.1 105.6 %copy-start.3 = (f32[55,2048]{1,0:T(8,128)S(1)}, f32[55,2048]{1,0:T(8,128)}, u32[]{:S(2)}) copy-start(f32[55,2048]{1,0:T(8,128)} %param.12) | copy-start | bytes 1351684
where the time goes:
time: 1420 us; the launch traced here: 1400 us
  other arithmetic  544 us (38%)
  local copies, waits for them, and re-layouts  440 us (31%)
  matrix products  136 us (10%)
  waiting for transfers between devices  113 us (8%)
  blocking collectives  96 us (7%)
  starting transfers between devices  44.1 us (3%)
  loops' own time  23.3 us (2%)
    scatter-add x2, other arithmetic, per_device(): jnp.zeros((field_count, local_count), jnp.float32).at[:, wanted]  197 us
    all_to_all x4, waiting for transfers between devices, route_rows(): lax.all_to_all(outgoing, ('gx', 'gy'), split_axis=1, concat_axis=1, tiled...  109 us
    gather x2, local copies, waits for them, and re-layouts, per_device(): reply = route_rows(params[:, wanted])  109 us
    psum x1, blocking collectives, per_device(): totals = lax.psum(jnp.stack(local_losses), ('gx', 'gy'))  96 us
    dot_general x96, matrix products, render(): jnp.dot(splat_rows[6:9], weight, precision=lax.Precision.HIGHEST, preferr...  87 us
    mul x64, other arithmetic, project(): opacity = 0.99 * jax.nn.sigmoid(gauss_rows[6])  76.1 us
    mul x32, other arithmetic, harmonics(): band_three[6] * ray_x * (sq_x - 3.0 * sq_y)  68.8 us
    add_any x32, other arithmetic, project(): screen_u = (gauss_rows[0] - camera_row[0]) / depth_z  67.5 us
  transfers between devices with their start and end apart: 6, of which 4 were waited for; matrix products, arithmetic and copies ran while one was open for 27% of the time, Pallas kernels for 0%

commit v1 on v0

v1 whole, which is shorter than its diff:
```python
import math

import jax
import jax.numpy as jnp
import numpy as np
from jax import lax
from jax.experimental import pallas as pl
from jax.experimental.pallas import tpu as pltpu
from jax.sharding import PartitionSpec as P

SIDE = 16
PIX = 256
NCOEF = 16
STEPS = 2
IMG_TX = 64
IMG_TY = 32
OWN = 128
LANES = 128
TILES_DEV = 16
LIST = 512
SLABS = LIST * TILES_DEV // 128
FIELDS = 9
F32 = jnp.float32
BF16 = jnp.bfloat16
I32 = jnp.int32

beta_one = 0.9
beta_two = 0.999
adam_eps = 1e-08
learn_rate = 0.01
adam_start = 1000
band_zero = 0.28209479177387814
band_one = 0.4886025119029199
band_two = (
    1.0925484305920792,
    -1.0925484305920792,
    0.31539156525252005,
    -1.0925484305920792,
    0.5462742152960396,
)
band_three = (
    -0.5900435899266435,
    2.890611442640554,
    -0.4570457994644658,
    0.3731763325901154,
    -0.4570457994644658,
    1.445305721320277,
    -0.5900435899266435,
)
half_log2e = math.sqrt(0.5 * math.log2(math.e))


def params_of(megabytes):
    return pltpu.CompilerParams(vmem_limit_bytes=megabytes << 20)


def harmonics(ray_x, ray_y, ray_z):
    sq_x = ray_x * ray_x
    sq_y = ray_y * ray_y
    sq_z = ray_z * ray_z
    return jnp.stack(
        [
            band_zero * jnp.ones_like(ray_x),
            -band_one * ray_y,
            band_one * ray_z,
            -band_one * ray_x,
            band_two[0] * ray_x * ray_y,
            band_two[1] * ray_y * ray_z,
            band_two[2] * (2.0 * sq_z - sq_x - sq_y),
            band_two[3] * ray_x * ray_z,
            band_two[4] * (sq_x - sq_y),
            band_three[0] * ray_y * (3.0 * sq_x - sq_y),
            band_three[1] * ray_x * ray_y * ray_z,
            band_three[2] * ray_y * (4.0 * sq_z - sq_x - sq_y),
            band_three[3] * ray_z * (2.0 * sq_z - 3.0 * sq_x - 3.0 * sq_y),
            band_three[4] * ray_x * (4.0 * sq_z - sq_x - sq_y),
            band_three[5] * ray_z * (sq_x - sq_y),
            band_three[6] * ray_x * (sq_x - 3.0 * sq_y),
        ]
    )


def project(gauss_rows, camera_row):
    image_width = 1.0 * SIDE * IMG_TX
    image_height = 1.0 * SIDE * IMG_TY
    depth_z = gauss_rows[2]
    screen_u = (gauss_rows[0] - camera_row[0]) / depth_z
    screen_v = (gauss_rows[1] - camera_row[1]) / depth_z
    inv_one = depth_z * depth_z * jnp.exp(-2.0 * gauss_rows[3])
    inv_two = depth_z * depth_z * jnp.exp(-2.0 * gauss_rows[4])
    cosine = jnp.cos(gauss_rows[5])
    sine_angle = jnp.sin(gauss_rows[5])
    conic_a = cosine * cosine * inv_one + sine_angle * sine_angle * inv_two
    conic_b = cosine * sine_angle * (inv_one - inv_two)
    conic_c = sine_angle * sine_angle * inv_one + cosine * cosine * inv_two
    log_opacity = math.log(0.99) - jax.nn.softplus(-gauss_rows[6])
    ray_x = (screen_u - 0.5 * image_width) / image_width
    ray_y = (screen_v - 0.5 * image_height) / image_width
    factor = lax.rsqrt(ray_x * ray_x + ray_y * ray_y + 1.0)
    harmonic_basis = harmonics(ray_x * factor, ray_y * factor, factor)
    coeffs = gauss_rows[7:].reshape(3, NCOEF, gauss_rows.shape[1])
    colour = 0.5 + jnp.sum(coeffs * harmonic_basis[None], axis=1)
    geometry = jnp.stack([screen_u, screen_v, conic_a, conic_b, conic_c, log_opacity])
    return jnp.concatenate([geometry, colour], 0), (inv_one, inv_two)


def factor_rows(projected, inverses):
    conic_a, conic_b, conic_c = projected[2], projected[3], projected[4]
    inv_one, inv_two = inverses
    has_a = conic_a > 0.0
    safe_a = jnp.where(has_a, conic_a, 1.0)
    root = jnp.sqrt(safe_a)
    alpha = jnp.where(has_a, half_log2e * root, 0.0)
    beta = jnp.where(has_a, half_log2e * conic_b / root, 0.0)
    gamma = half_log2e * jnp.where(
        has_a, jnp.sqrt(inv_one * (inv_two / safe_a)), jnp.sqrt(conic_c)
    )
    log2_opacity = jnp.maximum(projected[5] * math.log2(math.e), -1.0e4)
    return jnp.concatenate(
        [projected[0:2], jnp.stack([alpha, beta, gamma, log2_opacity]), projected[6:9]], 0
    )


def split3(values):
    hi = values.astype(BF16).astype(F32)
    rest = values - hi
    mid = rest.astype(BF16).astype(F32)
    return hi, mid, rest - mid


def routing_kernel(ids_ref, tx_ref, ty_ref, upper_ref, slot_ref, want_ref, tile_ref):
    row_iota = lax.broadcasted_iota(I32, (OWN, LANES), 0)
    zero = jnp.zeros((OWN, LANES), F32)
    upper = upper_ref[...]

    def body(k, carry):
        out = []
        for s in range(STEPS):
            counts, acc = carry[s]
            ids = ids_ref[s, pl.ds(k, 1), :]
            owner = lax.shift_right_logical(ids, 11)
            member = row_iota == owner
            member_bf = jnp.where(member, 1.0, 0.0).astype(BF16)
            ahead = jnp.dot(member_bf, upper, preferred_element_type=F32)
            rank = jnp.sum(
                jnp.where(member, ahead[:, :LANES] + counts, 0.0), axis=0, keepdims=True
            ).astype(I32)
            counts = counts + ahead[:, LANES:]
            slot_ref[s, pl.ds(k, 1), :] = owner * LANES + rank
            here = row_iota == rank
            local = ids & 2047
            cells = [
                jnp.where(here, value, 0.0).astype(BF16)
                for value in (
                    (local & 127).astype(F32),
                    lax.shift_right_logical(local, 7).astype(F32),
                    tx_ref[s, 0:1, :],
                    ty_ref[s, 0:1, :],
                )
            ]
            acc = acc + lax.dot_general(
                member_bf,
                jnp.concatenate(cells, 0),
                (((1,), (1,)), ((), ())),
                preferred_element_type=F32,
            )
            out.append((counts, acc))
        return tuple(out)

    start = tuple((zero, jnp.zeros((OWN, 4 * LANES), F32)) for _ in range(STEPS))
    done = lax.fori_loop(0, SLABS, body, start, unroll=2)
    for s in range(STEPS):
        acc = done[s][1].astype(I32)
        want_ref[s] = acc[:, 0:128] + acc[:, 128:256] * 128
        tile_ref[s] = acc[:, 256:384] + acc[:, 384:512] * IMG_TX


def routing(ids, tile_x, tile_y):
    strict = np.triu(np.ones((128, 128), np.float32), 1)
    upper = jnp.asarray(np.concatenate([strict, np.ones((128, 128), np.float32)], 1), BF16)
    return pl.pallas_call(
        routing_kernel,
        out_shape=(
            jax.ShapeDtypeStruct((STEPS, SLABS, LANES), I32),
            jax.ShapeDtypeStruct((STEPS, OWN, LANES), I32),
            jax.ShapeDtypeStruct((STEPS, OWN, LANES), I32),
        ),
        compiler_params=params_of(32),
        name="routing",
    )(ids, tile_x, tile_y, upper)


def gather_kernel(table_ref, want_ref, tile_ref, out_ref, shift_ref, parts, got):
    for f in range(FIELDS):
        for p, part in enumerate(split3(table_ref[f])):
            parts[f * 16 : f * 16 + 16, p * 128 : p * 128 + 128] = part.astype(BF16)
    low_iota = lax.broadcasted_iota(I32, (128, 256), 0)
    high_iota = lax.broadcasted_iota(I32, (16, 256), 0)

    def body(c, _):
        want = jnp.concatenate(
            [want_ref[pl.ds(2 * c, 1), :], want_ref[pl.ds(2 * c + 1, 1), :]], 1
        )
        hot = jnp.where(low_iota == (want & 127), 1.0, 0.0).astype(BF16)
        hot = jnp.concatenate([hot, hot, hot], 0)
        here = high_iota == lax.shift_right_logical(want, 7)
        picked = jnp.dot(parts[...], hot, preferred_element_type=F32)
        for f in range(FIELDS):
            row = jnp.sum(
                jnp.where(here, picked[f * 16 : f * 16 + 16], 0.0), axis=0, keepdims=True
            )
            got[f, pl.ds(2 * c, 1), :] = row[:, :128]
            got[f, pl.ds(2 * c + 1, 1), :] = row[:, 128:]
        return 0

    lax.fori_loop(0, OWN // 2, body, 0, unroll=2)
    tile = tile_ref[...]
    centre_x = ((tile & (IMG_TX - 1)) * SIDE + SIDE // 2).astype(F32)
    centre_y = (lax.shift_right_logical(tile, 6) * SIDE + SIDE // 2).astype(F32)
    local_u = got[0] - centre_x
    local_v = got[1] - centre_y
    shift_ref[0] = local_u
    shift_ref[1] = local_v
    alpha, beta, gamma = got[2], got[3], got[4]
    out_ref[0] = alpha
    out_ref[1] = beta
    out_ref[2] = gamma
    out_ref[3] = -(alpha * local_u + beta * local_v)
    out_ref[4] = -gamma * local_v
    for f in range(5, FIELDS):
        out_ref[f] = got[f]


def owner_gather(table, want, tile):
    return pl.pallas_call(
        gather_kernel,
        out_shape=(
            jax.ShapeDtypeStruct((FIELDS, OWN, LANES), F32),
            jax.ShapeDtypeStruct((2, OWN, LANES), F32),
        ),
        scratch_shapes=[
            pltpu.VMEM((FIELDS * 16, 384), BF16),
            pltpu.VMEM((FIELDS, OWN, LANES), F32),
        ],
        compiler_params=params_of(32),
        name="owner_gather",
    )(table, want, tile)


def scatter_kernel(moment_ref, shift_ref, want_ref, out_ref, high, rest):
    local_u, local_v = shift_ref[0], shift_ref[1]
    m0, mx, my = moment_ref[0], moment_ref[1], moment_ref[2]
    sx = mx - local_u * m0
    sy = my - local_v * m0
    sums = [
        sx,
        sy,
        moment_ref[3] - local_u * (mx + sx),
        moment_ref[4] - local_u * my - local_v * sx,
        moment_ref[5] - local_v * (my + sy),
        m0,
        moment_ref[6],
        moment_ref[7],
        moment_ref[8],
    ]
    for f in range(FIELDS):
        top = sums[f].astype(BF16).astype(F32)
        high[f] = top
        rest[f] = sums[f] - top
    low_iota = lax.broadcasted_iota(I32, (128, 128), 0)
    high_iota = lax.broadcasted_iota(I32, (16, 128), 0)

    def body(c, acc):
        lefts, rights = [], []
        for half in range(2):
            d = 2 * c + half
            want = want_ref[pl.ds(d, 1), :]
            rights.append(jnp.where(low_iota == (want & 127), 1.0, 0.0).astype(BF16))
            here = high_iota == lax.shift_right_logical(want, 7)
            rows = [
                jnp.where(here, ref[f, pl.ds(d, 1), :], 0.0).astype(BF16)
                for ref in (high, rest)
                for f in range(FIELDS)
            ]
            lefts.append(jnp.concatenate(rows, 0))
        return acc + lax.dot_general(
            jnp.concatenate(lefts, 1),
            jnp.concatenate(rights, 1),
            (((1,), (1,)), ((), ())),
            preferred_element_type=F32,
        )

    acc = lax.fori_loop(
        0, OWN // 2, body, jnp.zeros((2 * FIELDS * 16, 128), F32), unroll=2
    )
    out_ref[...] = acc[: FIELDS * 16] + acc[FIELDS * 16 :]


def owner_scatter(moments, shifts, want):
    return pl.pallas_call(
        scatter_kernel,
        out_shape=jax.ShapeDtypeStruct((FIELDS * 16, 128), F32),
        scratch_shapes=[
            pltpu.VMEM((FIELDS, OWN, LANES), F32),
            pltpu.VMEM((FIELDS, OWN, LANES), F32),
        ],
        compiler_params=params_of(32),
        name="owner_scatter",
    )(moments, shifts, want)


def render_constants():
    axis = np.arange(SIDE, dtype=np.float32) - 7.5
    x = np.tile(axis, SIDE)
    y = np.repeat(axis, SIDE)
    one = np.ones_like(x)
    zero = np.zeros_like(x)
    block = np.zeros((8, 512), np.float32)
    block[0] = np.concatenate([x, zero])
    block[1] = np.concatenate([y, zero])
    block[2] = np.concatenate([zero, y])
    block[3] = np.concatenate([one, zero])
    block[4] = np.concatenate([zero, one])
    lines = np.concatenate([block, block, block, np.zeros_like(block)], 0)
    mono = np.zeros((PIX, 128), np.float32)
    for k, column in enumerate((one, x, y, x * x, x * y, y * y)):
        mono[:, k] = column
    return jnp.asarray(lines, BF16), jnp.asarray(mono, BF16)


COL_OPACITY = 29


def render_kernel(
    slot_ref, fields_ref, target_ref, lines_ref, mono_ref,
    picture_ref, moment_ref, loss_ref,
    table, rows, line_a, line_b, alphas, weights, out_a, out_b, resid, back,
):
    def build(o, _):
        first = fields_ref[0:8, pl.ds(o, 1), :].reshape(8, LANES)
        last = jnp.broadcast_to(fields_ref[8, pl.ds(o, 1), :], (8, LANES))
        stack = jnp.concatenate([*split3(first), first, last], 0)
        table[pl.ds(pl.multiple_of(o * 128, 128), 128), 0:40] = stack.T
        return 0

    lax.fori_loop(0, OWN, build, 0, unroll=4)

    def zero_out(o, _):
        back[pl.ds(pl.multiple_of(o * 128, 128), 128), :] = jnp.zeros((128, LANES), F32)
        return 0

    lax.fori_loop(0, OWN, zero_out, 0)

    def fetch(slab, i):
        source = jnp.minimum(slab, SLABS - 1)
        for t in range(TILES_DEV):
            q = i * TILES_DEV + t
            rows[pl.ds(pl.multiple_of(slab * 128, 128) + q, 1), :] = table[
                pl.ds(slot_ref[source * 128 + q], 1), :
            ]

    def lines_of(slab, line):
        left = rows[pl.ds(pl.multiple_of(slab * 128, 128), 128), 0:32].astype(BF16)
        line[...] = jnp.dot(left, lines_ref[...], preferred_element_type=F32)

    def forward(slab, line, state):
        through, red, green, blue = state
        for i in range(8):
            at = pl.ds(pl.multiple_of(slab * 128, 128) + i * 16, 16)
            first = line[i * 16 : i * 16 + 16, 0:256]
            second = line[i * 16 : i * 16 + 16, 256:512]
            cols = rows[at, COL_OPACITY : COL_OPACITY + 4]
            alpha = jnp.exp2(cols[:, 0:1] - first * first - second * second)
            weight = through * alpha
            through = through - weight
            red = red + weight * cols[:, 1:2]
            green = green + weight * cols[:, 2:3]
            blue = blue + weight * cols[:, 3:4]
            alphas[at, :] = alpha
            weights[at, :] = weight
            fetch(slab + 2, i)
        return through, red, green, blue

    for slab in range(2):
        for i in range(8):
            fetch(slab, i)
    lines_of(0, line_a)

    def forward_pair(pair, state):
        lines_of(2 * pair + 1, line_b)
        state = forward(2 * pair, line_a, state)
        lines_of(2 * pair + 2, line_a)
        return forward(2 * pair + 1, line_b, state)

    blank = jnp.zeros((TILES_DEV, PIX), F32)
    _, red, green, blue = lax.fori_loop(
        0, SLABS // 2, forward_pair, (jnp.ones((TILES_DEV, PIX), F32), blank, blank, blank)
    )
    residuals = []
    total = jnp.zeros((), F32)
    for ch, colour in enumerate((red, green, blue)):
        picture_ref[ch] = colour
        residual = colour - target_ref[ch]
        residuals.append(residual)
        total = total + jnp.sum(residual * residual)
    loss_ref[...] = jnp.full((1, LANES), 0.5 * total, F32)
    res_red, res_green, res_blue = residuals

    padded = jnp.concatenate([jnp.zeros((16, PIX), F32), *residuals, jnp.zeros((64, PIX), F32)], 0)
    turned = padded.T
    top = turned.astype(BF16)
    resid[:, 0:128] = top
    resid[:, 128:256] = (turned - top.astype(F32)).astype(BF16)

    lane = lax.broadcasted_iota(I32, (128, LANES), 1)
    row = lax.broadcasted_iota(I32, (128, LANES), 0)
    own_tile = (lane & 15) == (row & 15)

    def scatter(slab, i, source):
        for t in range(TILES_DEV):
            q = i * TILES_DEV + t
            back[pl.ds(slot_ref[slab * 128 + q], 1), :] = source[q : q + 1, :]

    def backward(slab, behind, target, previous, source):
        pieces = [None] * 8
        for i in range(7, -1, -1):
            at = pl.ds(pl.multiple_of(slab * 128, 128) + i * 16, 16)
            cols = rows[at, COL_OPACITY : COL_OPACITY + 4]
            alpha = alphas[at, :]
            gain = (
                res_red * cols[:, 1:2] + res_green * cols[:, 2:3] + res_blue * cols[:, 3:4]
            ) - behind
            pieces[i] = weights[at, :] * gain
            behind = behind + alpha * gain
            if source is not None:
                scatter(previous, i, source)
        slope = jnp.concatenate(pieces, 0)
        slope_top = slope.astype(BF16)
        slope_rest = (slope - slope_top.astype(F32)).astype(BF16)
        weight = weights[pl.ds(pl.multiple_of(slab * 128, 128), 128), :]
        weight_top = weight.astype(BF16)
        weight_rest = (weight - weight_top.astype(F32)).astype(BF16)
        moment = jnp.dot(slope_top, mono_ref[...], preferred_element_type=F32)
        moment = moment + jnp.dot(slope_rest, mono_ref[...], preferred_element_type=F32)
        both = jnp.dot(weight_top, resid[...], preferred_element_type=F32)
        shade = both[:, :128] + both[:, 128:]
        shade = shade + jnp.dot(weight_rest, resid[:, 0:128], preferred_element_type=F32)
        target[...] = moment + jnp.where(own_tile, shade, 0.0)
        return behind

    behind = backward(SLABS - 1, blank, out_a, None, None)

    def backward_pair(pair, behind):
        slab = SLABS - 2 - 2 * pair
        behind = backward(slab, behind, out_b, slab + 1, out_a)
        return backward(slab - 1, behind, out_a, slab, out_b)

    behind = lax.fori_loop(0, SLABS // 2 - 1, backward_pair, behind)
    backward(0, behind, out_b, 1, out_a)
    for i in range(8):
        scatter(0, i, out_b)

    def finish(o, _):
        turned = back[pl.ds(pl.multiple_of(o * 128, 128), 128), 0:64].T
        for k in range(6):
            moment_ref[k, pl.ds(o, 1), :] = turned[k : k + 1]
        for ch in range(3):
            part = turned[16 + 16 * ch : 32 + 16 * ch]
            moment_ref[6 + ch, pl.ds(o, 1), :] = jnp.sum(part, axis=0, keepdims=True)
        return 0

    lax.fori_loop(0, OWN, finish, 0, unroll=4)


def render(slots, fields, target):
    lines, mono = render_constants()
    vmem = pl.BlockSpec(memory_space=pltpu.VMEM)
    entries = SLABS * 128
    return pl.pallas_call(
        render_kernel,
        out_shape=(
            jax.ShapeDtypeStruct((3, TILES_DEV, PIX), F32),
            jax.ShapeDtypeStruct((FIELDS, OWN, LANES), F32),
            jax.ShapeDtypeStruct((1, LANES), F32),
        ),
        in_specs=[pl.BlockSpec(memory_space=pltpu.SMEM)] + [vmem] * 4,
        out_specs=(vmem, vmem, vmem),
        scratch_shapes=[
            pltpu.VMEM((OWN * LANES, LANES), F32),
            pltpu.VMEM((entries + 256, LANES), F32),
            pltpu.VMEM((128, 512), F32),
            pltpu.VMEM((128, 512), F32),
            pltpu.VMEM((entries, PIX), F32),
            pltpu.VMEM((entries, PIX), F32),
            pltpu.VMEM((128, LANES), F32),
            pltpu.VMEM((128, LANES), F32),
            pltpu.VMEM((PIX, 256), BF16),
            pltpu.VMEM((OWN * LANES, LANES), F32),
        ],
        compiler_params=params_of(56),
        name="render",
    )(slots, fields, target, lines, mono)


def exchange(blocks):
    return lax.all_to_all(blocks, ("gx", "gy"), split_axis=1, concat_axis=1, tiled=True)


def adam_update(params, moment_one, second, gradient, step_index):
    step_count = adam_start + step_index + 1
    moment_one = beta_one * moment_one + (1.0 - beta_one) * gradient
    second = beta_two * second + (1.0 - beta_two) * gradient * gradient
    scaled_first = moment_one / (1.0 - beta_one**step_count)
    scaled_second = second / (1.0 - beta_two**step_count)
    params = params - learn_rate * scaled_first / (jnp.sqrt(scaled_second) + adam_eps)
    return (params, moment_one, second)


def per_device(gauss_params, first_moment, second_moment, splat_lists, tile_ids, targets, camera):
    local_count = gauss_params.shape[1]
    params, moment_one, moment_two = (gauss_params, first_moment, second_moment)
    ids = jnp.swapaxes(splat_lists, 1, 2).reshape(STEPS, SLABS, LANES)
    lane_tiles = jnp.tile(tile_ids, (1, LANES // TILES_DEV))
    tile_x = (lane_tiles % IMG_TX).astype(F32)[:, None, :]
    tile_y = (lane_tiles // IMG_TX).astype(F32)[:, None, :]
    slots, want, tiles = routing(ids, tile_x, tile_y)
    slots = slots.reshape(STEPS, SLABS * LANES)
    asked = exchange(jnp.concatenate([want, tiles], 0))
    pictures = []
    losses = []
    for step_index in range(STEPS):
        wanted, wanted_tile = asked[step_index], asked[STEPS + step_index]
        projected, pullback, inverses = jax.vjp(
            lambda values: project(values, camera[step_index]), params, has_aux=True
        )
        table = factor_rows(projected, inverses).reshape(FIELDS, 16, 128)
        fields, shifts = owner_gather(table, wanted, wanted_tile)
        fields = exchange(fields)
        target = jnp.swapaxes(targets[step_index], 0, 1)
        picture, moments, loss = render(slots[step_index], fields, target)
        extra = jnp.broadcast_to(loss[None], (1, OWN, LANES))
        arrived = exchange(jnp.concatenate([moments, extra], 0))
        losses.append(jnp.sum(arrived[FIELDS, :, 0]))
        sums = owner_scatter(arrived, shifts, wanted).reshape(FIELDS, local_count)
        conic_a, conic_b, conic_c = projected[2], projected[3], projected[4]
        cotangent = jnp.concatenate(
            [
                jnp.stack(
                    [
                        conic_a * sums[0] + conic_b * sums[1],
                        conic_b * sums[0] + conic_c * sums[1],
                        -0.5 * sums[2],
                        -sums[3],
                        -0.5 * sums[4],
                    ]
                ),
                sums[5:9],
            ],
            0,
        )
        gradient = pullback(cotangent)[0]
        params, moment_one, moment_two = adam_update(
            params, moment_one, moment_two, gradient, step_index
        )
        pictures.append(jnp.swapaxes(picture, 0, 1))
    loss_values = jnp.stack(losses) / (3.0 * PIX * TILES_DEV * OWN)
    return (params, moment_one, moment_two, jnp.stack(pictures), loss_values)


def solution(mesh):
    both = ("gx", "gy")
    in_specs = (
        P(None, both),
        P(None, both),
        P(None, both),
        P(None, both, None),
        P(None, both),
        P(None, both, None, None),
        P(),
    )
    out_specs = (
        P(None, both),
        P(None, both),
        P(None, both),
        P(None, both, None, None),
        P(),
    )
    return jax.shard_map(
        per_device, mesh=mesh, in_specs=in_specs, out_specs=out_specs, check_vma=False
    )
```

time: 1420 us -> 298 us (0.21); the launches traced: 1400 us -> 297 us
  other arithmetic: 544 us -> 18 us
  local copies, waits for them, and re-layouts: 440 us -> 14.9 us
  Pallas kernels: 0 us -> 154 us
  matrix products: 136 us -> 0 us
  waiting for transfers between devices: 113 us -> 42.1 us
  blocking collectives: 96 us -> 46.6 us
  starting transfers between devices: 44.1 us -> 20.6 us
  loops' own time: 23.3 us -> 0 us
    scatter-add x2 -> x0, other arithmetic: 197 us -> none  [per_device(): jnp.zeros((field_count, local_count), jnp.float32).at[:, wanted]]
    mul x226 -> x4, other arithmetic: 177 us -> 0.7 us  [the longest x2 0.69 us: factor_rows(): half_log2e * jnp.where(has_a, jnp.sqrt(inv_one * (inv_two / safe_a)), jnp...]
    gather x4 -> x0, local copies, waits for them, and re-layouts: 171 us -> none  [the longest x2 109 us: per_device(): reply = route_rows(params[:, wanted])]
    pallas_call x0 -> x7, Pallas kernels: none -> 154 us  [the longest x2 84 us: render(): pl.pallas_call(render_kernel, out_shape=(jax.ShapeDtypeStruct((3, TILES_D...]
    dot_general x162 -> x0, matrix products: 136 us -> none  [the longest x96 87 us: render(): jnp.dot(splat_rows[6:9], weight, precision=lax.Precision.HIGHEST, preferr...]
    scatter x4 -> x0, local copies, waits for them, and re-layouts: 112 us -> none  [the longest x2 62.1 us: per_device(): jnp.zeros((owners * capacity,), jnp.int32).at[slot_pos].set(local_id)]
    psum x1 -> x0, blocking collectives: 96 us -> none  [per_device(): totals = lax.psum(jnp.stack(local_losses), ('gx', 'gy'))]
    all_to_all x6 -> x3, waiting for transfers between devices: 113 us -> 42.1 us  [exchange(): lax.all_to_all(blocks, ('gx', 'gy'), split_axis=1, concat_axis=1, tiled=T...]
  transfers between devices with their start and end apart: 6 -> 3, of which waited for: 4 -> 3; matrix products, arithmetic and copies ran while one was open for 27% -> 2% of each run, Pallas kernels for 0% -> 0%
where the time goes in v1:
time: 298 us; the launch traced here: 297 us
  Pallas kernels  154 us (52%)
  blocking collectives  46.6 us (16%)
  waiting for transfers between devices  42.1 us (14%)
  starting transfers between devices  20.6 us (7%)
  other arithmetic  18 us (6%)
  local copies, waits for them, and re-layouts  14.9 us (5%)
    pallas_call x2, Pallas kernels, render(): pl.pallas_call(render_kernel, out_shape=(jax.ShapeDtypeStruct((3, TILES_D...  84 us
    all_to_all x2, blocking collectives, exchange(): lax.all_to_all(blocks, ('gx', 'gy'), split_axis=1, concat_axis=1, tiled=T...  46.6 us
    all_to_all x3, waiting for transfers between devices, exchange(): lax.all_to_all(blocks, ('gx', 'gy'), split_axis=1, concat_axis=1, tiled=T...  42.1 us
    pallas_call x1, Pallas kernels, routing(): pl.pallas_call(routing_kernel, out_shape=(jax.ShapeDtypeStruct((STEPS, SL...  37 us
    all_to_all x3, starting transfers between devices, exchange(): lax.all_to_all(blocks, ('gx', 'gy'), split_axis=1, concat_axis=1, tiled=T...  20.6 us
    pallas_call x2, Pallas kernels, owner_gather(): pl.pallas_call(gather_kernel, out_shape=(jax.ShapeDtypeStruct((FIELDS, OW...  16.7 us
    pallas_call x2, Pallas kernels, owner_scatter(): pl.pallas_call(scatter_kernel, out_shape=jax.ShapeDtypeStruct((FIELDS * 1...  15.9 us
  transfers between devices with their start and end apart: 3, of which 3 were waited for; matrix products, arithmetic and copies ran while one was open for 2% of the time, Pallas kernels for 0%

profile of v1, /device:TPU:1, one launch (start us, length us, event | category | flops | bytes accessed | tf_op | source)
XLA Modules:
  0.0 297.0 jit_solution(8709979728940564603)
XLA Ops:
  0.6 0.7 tile.4
  1.4 1.0 copy.19
  2.7 0.6 copy-done
  3.3 37.0 %routing.1 = (s32[2,64,128]{2,1,0:T(8,128)S(1)}, s32[2,128,128]{2,1,0:T(8,128)S(1)}, s32[2,128,128]{2,1,0:T(8,128)S(1)}) custom-call(s32[2,64,128]{2,1,0:T(8,128)S(1)} %reshape.325.ids_ref, f32[2,1,128]{2,1,0:T(1,128)S(1)} %fusion.54.tx_ref, f32[2,1,128]{2,1,0:T(1,128)S(1)} %get-tuple-element.86.ty_ref, bf16[128,256]{1,0:T(8,128)(2,1)S(1)} %copy-done), custom_call_target="tpu_custom_call" | custom-call | tf_op jit(solution)/shard_map/routing/pallas_call | solution.py:181
  40.4 0.9 copy.20
  41.2 11.5 %all-to-all-start = ((s32[4,128,128]{2,0,1:T(4,128)}), s32[4,128,128]{2,0,1:T(4,128)S(1)}, u32[]{:S(2)}, u32[]{:S(2)}) async-start(s32[4,128,128]{2,0,1:T(4,128)} %copy.20), calls=%async_computation | async-start | bytes 524288 | tf_op jit(solution)/shard_map/all_to_all | solution.py:506
  53.1 0.6 copy-done.13
  53.8 0.7 fusion.86
  54.4 1.7 multiply_select_fusion.2
  56.6 7.2 %all-to-all-done = s32[4,128,128]{2,0,1:T(4,128)S(1)} async-done(((s32[4,128,128]{2,0,1:T(4,128)}), s32[4,128,128]{2,0,1:T(4,128)S(1)}, u32[]{:S(2)}, u32[]{:S(2)}) %all-to-all-start) | async-done | bytes 262176 | tf_op jit(solution)/shard_map/all_to_all | solution.py:506
  64.0 8.3 %owner_gather.2 = (f32[9,128,128]{2,1,0:T(8,128)S(1)}, f32[2,128,128]{2,1,0:T(8,128)S(1)}) custom-call(f32[9,16,128]{2,1,0:T(8,128)S(1)} %constant_dynamic-update-slice_fusion.table_ref, s32[128,128]{1,0:T(8,128)S(1)} %bitcast.119, s32[128,128]{1,0:T(8,128)S(1)} %bitcast.122), custom_call_target="tpu_custom_call" | custom-call | tf_op jit(solution)/shard_map/owner_gather/pallas_call | solution.py:235
  72.4 1.4 copy.23
  73.7 4.3 %all-to-all-start.1 = ((f32[9,128,128]{2,0,1:T(8,128)}), f32[9,128,128]{2,0,1:T(8,128)S(1)}, u32[]{:S(2)}, u32[]{:S(2)}) async-start(f32[9,128,128]{2,0,1:T(8,128)} %copy.23), calls=%async_computation.1 | async-start | bytes 2097152 | tf_op jit(solution)/shard_map/all_to_all | solution.py:506
  78.0 0.6 slice_bitcast_fusion.2
  79.0 0.6 slice_bitcast_fusion
  79.6 17.3 %all-to-all-done.1 = f32[9,128,128]{2,0,1:T(8,128)S(1)} async-done(((f32[9,128,128]{2,0,1:T(8,128)}), f32[9,128,128]{2,0,1:T(8,128)S(1)}, u32[]{:S(2)}, u32[]{:S(2)}) %all-to-all-start.1) | async-done | bytes 589856 | tf_op jit(solution)/shard_map/all_to_all | solution.py:506
  96.9 1.0 copy.24.fields_ref
  97.9 42.0 %render.2 = (f32[3,16,256]{2,1,0:T(8,128)}, f32[9,128,128]{2,1,0:T(8,128)}, f32[1,128]{1,0:T(1,128)}) custom-call(s32[8192]{0:T(1024)} %get-tuple-element.131.slot_ref, f32[9,128,128]{2,1,0:T(8,128)} %copy.24.fields_ref, f32[3,16,256]{2,1,0:T(8,128)} %get-tuple-element.119.target_ref, bf16[32,512]{1,0:T(8,128)(2,1)} %constant.132.clone.lines_ref, ...), custom_call_target="tpu_custom_call" | custom-call | tf_op jit(solution)/shard_map/render/pallas_call | solution.py:479
  139.9 0.6 copy-done.15
  140.6 1.1 pad_maximum_fusion
  141.7 0.4 copy.25
  142.1 23.3 %all_to_all.25 = f32[10,128,128]{2,0,1:T(8,128)S(1)} all-to-all(f32[10,128,128]{2,0,1:T(8,128)S(1)} %copy.25), channel_id=1, replica_groups=mesh['gx'=4,'gy'=32] {'gx','gy'}, dimensions={1} | all-to-all | bytes 1310720 | tf_op jit(solution)/shard_map/all_to_all | solution.py:506
  165.6 7.9 %owner_scatter.2 = f32[144,128]{1,0:T(8,128)S(1)} custom-call(f32[10,128,128]{2,1,0:T(8,128)S(1)} %copy.26.moment_ref, f32[2,128,128]{2,1,0:T(8,128)S(1)} %get-tuple-element.29.shift_ref, s32[128,128]{1,0:T(8,128)S(1)} %bitcast.120), custom_call_target="tpu_custom_call" | custom-call | tf_op jit(solution)/shard_map/owner_scatter/pallas_call | solution.py:300
  173.7 0.6 slice_divide_fusion.3
  174.6 0.4 fusion.2
  175.0 1.4 fusion.12
  176.4 0.5 divide_subtract_fusion.1
  177.3 0.5 copy-done.9
  177.8 1.5 multiply_select_fusion
  179.9 8.3 %owner_gather.3 = (f32[9,128,128]{2,1,0:T(8,128)S(1)}, f32[2,128,128]{2,1,0:T(8,128)S(1)}) custom-call(f32[9,16,128]{2,1,0:T(8,128)S(1)} %constant_dynamic-update-slice_fusion.7.table_ref, s32[128,128]{1,0:T(8,128)S(1)} %bitcast.117, s32[128,128]{1,0:T(8,128)S(1)} %bitcast.121), custom_call_target="tpu_custom_call" | custom-call | tf_op jit(solution)/shard_map/owner_gather/pallas_call | solution.py:235
  188.3 0.4 copy.29
  188.6 23.3 %all_to_all.26 = f32[9,128,128]{2,0,1:T(8,128)S(1)} all-to-all(f32[9,128,128]{2,0,1:T(8,128)S(1)} %copy.29), channel_id=1, replica_groups=mesh['gx'=4,'gy'=32] {'gx','gy'}, dimensions={1} | all-to-all | bytes 1179648 | tf_op jit(solution)/shard_map/all_to_all | solution.py:506
  211.9 1.0 copy.30.fields_ref
  212.9 42.0 %render.3 = (f32[3,16,256]{2,1,0:T(8,128)}, f32[9,128,128]{2,1,0:T(8,128)}, f32[1,128]{1,0:T(1,128)}) custom-call(s32[8192]{0:T(1024)} %get-tuple-element.130.slot_ref, f32[9,128,128]{2,1,0:T(8,128)} %copy.30.fields_ref, f32[3,16,256]{2,1,0:T(8,128)} %get-tuple-element.118.target_ref, bf16[32,512]{1,0:T(8,128)(2,1)} %constant.132.clone.lines_ref, ...), custom_call_target="tpu_custom_call" | custom-call | tf_op jit(solution)/shard_map/render/pallas_call | solution.py:479
  254.9 0.7 copy-done.14
  255.5 1.1 pad_maximum_fusion.1
  256.7 1.4 copy.31
  258.0 4.8 %all-to-all-start.4 = ((f32[10,128,128]{2,0,1:T(8,128)}), f32[10,128,128]{2,0,1:T(8,128)S(1)}, u32[]{:S(2)}, u32[]{:S(2)}) async-start(f32[10,128,128]{2,0,1:T(8,128)} %copy.31), calls=%async_computation.4 | async-start | bytes 2097152 | tf_op jit(solution)/shard_map/all_to_all | solution.py:506
  262.9 0.8 slice_reduce_fusion.1
  263.7 0.6 pad_maximum_fusion.2
  264.3 17.6 %all-to-all-done.4 = f32[10,128,128]{2,0,1:T(8,128)S(1)} async-done(((f32[10,128,128]{2,0,1:T(8,128)}), f32[10,128,128]{2,0,1:T(8,128)S(1)}, u32[]{:S(2)}, u32[]{:S(2)}) %all-to-all-start.4) | async-done | bytes 655392 | tf_op jit(solution)/shard_map/all_to_all | solution.py:506
  282.1 7.9 %owner_scatter.3 = f32[144,128]{1,0:T(8,128)S(1)} custom-call(f32[10,128,128]{2,1,0:T(8,128)S(1)} %copy.32.moment_ref, f32[2,128,128]{2,1,0:T(8,128)S(1)} %get-tuple-element.35.shift_ref, s32[128,128]{1,0:T(8,128)S(1)} %bitcast.118), custom_call_target="tpu_custom_call" | custom-call | tf_op jit(solution)/shard_map/owner_scatter/pallas_call | solution.py:300
  290.3 0.7 slice_reduce_fusion
  291.0 1.8 maximum_multiply_fusion
  292.8 0.6 slice_divide_fusion.1
  293.8 0.4 fusion.13
  294.1 1.3 fusion.23
  295.4 1.6 divide_subtract_fusion
  (76 shorter events, 3.8 us)
Async XLA Ops:
  2.5 0.8 copy-start
  40.3 12.4 %copy-start.3 = (f32[55,2048]{1,0:T(8,128)S(1)}, f32[55,2048]{1,0:T(8,128)}, u32[]{:S(2)}) copy-start(f32[55,2048]{1,0:T(8,128)} %param.13) | copy-start | bytes 1351684
  41.2 22.6 %all-to-all-start = ((s32[4,128,128]{2,0,1:T(4,128)}), s32[4,128,128]{2,0,1:T(4,128)S(1)}, u32[]{:S(2)}, u32[]{:S(2)}) async-start(s32[4,128,128]{2,0,1:T(4,128)} %copy.20), calls=%async_computation | async-start | bytes 524288 | tf_op jit(solution)/shard_map/all_to_all | solution.py:506
  53.1 0.7 copy-start.13
  73.7 23.2 %all-to-all-start.1 = ((f32[9,128,128]{2,0,1:T(8,128)}), f32[9,128,128]{2,0,1:T(8,128)S(1)}, u32[]{:S(2)}, u32[]{:S(2)}) async-start(f32[9,128,128]{2,0,1:T(8,128)} %copy.23), calls=%async_computation.1 | async-start | bytes 2097152 | tf_op jit(solution)/shard_map/all_to_all | solution.py:506
  78.0 0.9 copy-start.8
  139.9 0.6 copy-start.15
  173.6 2.8 copy-start.6
  173.7 2.7 copy-start.4
  177.2 0.6 copy-start.9
  177.3 2.5 copy-start.1
  254.9 0.7 copy-start.14
  258.0 5.6 %copy-start.12 = (f32[3,16,256]{2,1,0:T(8,128)S(1)}, f32[3,16,256]{2,1,0:T(8,128)}, u32[]{:S(2)}) copy-start(f32[3,16,256]{2,1,0:T(8,128)} %get-tuple-element.38) | copy-start | bytes 147460
  258.0 23.8 %all-to-all-start.4 = ((f32[10,128,128]{2,0,1:T(8,128)}), f32[10,128,128]{2,0,1:T(8,128)S(1)}, u32[]{:S(2)}, u32[]{:S(2)}) async-start(f32[10,128,128]{2,0,1:T(8,128)} %copy.31), calls=%async_computation.4 | async-start | bytes 2097152 | tf_op jit(solution)/shard_map/all_to_all | solution.py:506
  262.9 0.8 copy-start.11
  282.1 8.0 %copy-start.2 = (f32[48,2048]{1,0:T(8,128)S(1)}, f32[48,2048]{1,0:T(8,128)}, u32[]{:S(2)}) copy-start(f32[48,2048]{1,0:T(8,128)} %copy-done.1) | copy-start | bytes 1179652
  290.2 3.3 %copy-start.10 = (f32[1,2048]{1,0:T(1,128)S(1)}, f32[1,2048]{1,0:T(1,128)}, u32[]{:S(2)}) copy-start(f32[1,2048]{1,0:T(1,128)} %copy-done.9) | copy-start | bytes 24580
  290.2 5.2 %copy-start.7 = (f32[55,2048]{1,0:T(8,128)S(1)}, f32[55,2048]{1,0:T(8,128)}, u32[]{:S(2)}) copy-start(f32[55,2048]{1,0:T(8,128)} %param.15) | copy-start | bytes 1351684
  290.2 5.2 %copy-start.5 = (f32[55,2048]{1,0:T(8,128)S(1)}, f32[55,2048]{1,0:T(8,128)}, u32[]{:S(2)}) copy-start(f32[55,2048]{1,0:T(8,128)} %param.14) | copy-start | bytes 1351684

commit v2 on v1

--- a/solution.py
+++ b/solution.py
@@ -1,3 +1,4 @@
+import functools
 import math
 
 import jax
@@ -128,8 +129,78 @@
     return hi, mid, rest - mid
 
 
-def routing_kernel(ids_ref, tx_ref, ty_ref, upper_ref, slot_ref, want_ref, tile_ref):
+def my_index():
+    return lax.axis_index("gx") * lax.axis_size("gy") + lax.axis_index("gy")
+
+
+def mesh_place(device):
+    inner = lax.axis_size("gy")
+    return (device // inner, lax.rem(device, inner))
+
+
+def greet():
+    barrier = pltpu.get_barrier_semaphore()
+    me = my_index()
+
+    def one(k, _):
+        pl.semaphore_signal(
+            barrier,
+            inc=1,
+            device_id=mesh_place(lax.rem(me + k, OWN)),
+            device_id_type=pl.DeviceIdType.MESH,
+        )
+        return 0
+
+    lax.fori_loop(1, OWN, one, 0, unroll=2)
+
+
+def all_entered():
+    pl.semaphore_wait(pltpu.get_barrier_semaphore(), OWN - 1)
+
+
+def send(source, target, peer, send_sem, recv_sem):
+    me = my_index()
+    pltpu.make_async_remote_copy(
+        src_ref=source.at[:, peer, :],
+        dst_ref=target.at[:, me, :],
+        send_sem=send_sem,
+        recv_sem=recv_sem,
+        device_id=mesh_place(peer),
+        device_id_type=pl.DeviceIdType.MESH,
+    ).start()
+
+
+def all_but_one(source, target, send_sem, recv_sem):
+    blocks = pl.ds(0, OWN - 1)
+    return pltpu.make_async_remote_copy(
+        src_ref=source.at[:, blocks, :],
+        dst_ref=target.at[:, blocks, :],
+        send_sem=send_sem,
+        recv_sem=recv_sem,
+        device_id=mesh_place(my_index()),
+        device_id_type=pl.DeviceIdType.MESH,
+    )
+
+
+def keep_own(source, target):
+    me = my_index()
+    for k in range(source.shape[0]):
+        target[k, pl.ds(me, 1), :] = source[k, pl.ds(me, 1), :]
+
+
+def remote_params(collective_id, megabytes=32):
+    return pltpu.CompilerParams(
+        collective_id=collective_id, has_side_effects=True, vmem_limit_bytes=megabytes << 20
+    )
+
+
+GROUP = 4
+
+
+def routing_kernel(ids_ref, tile_ref, upper_ref, slot_ref, asked_ref, request, send_sem, recv_sem):
+    greet()
     row_iota = lax.broadcasted_iota(I32, (OWN, LANES), 0)
+    own_tile = (lax.broadcasted_iota(I32, (1, LANES), 1) & (TILES_DEV - 1)).astype(F32)
     zero = jnp.zeros((OWN, LANES), F32)
     upper = upper_ref[...]
 
@@ -137,176 +208,317 @@
         out = []
         for s in range(STEPS):
             counts, acc = carry[s]
-            ids = ids_ref[s, pl.ds(k, 1), :]
-            owner = lax.shift_right_logical(ids, 11)
-            member = row_iota == owner
-            member_bf = jnp.where(member, 1.0, 0.0).astype(BF16)
-            ahead = jnp.dot(member_bf, upper, preferred_element_type=F32)
-            rank = jnp.sum(
-                jnp.where(member, ahead[:, :LANES] + counts, 0.0), axis=0, keepdims=True
-            ).astype(I32)
-            counts = counts + ahead[:, LANES:]
-            slot_ref[s, pl.ds(k, 1), :] = owner * LANES + rank
-            here = row_iota == rank
-            local = ids & 2047
-            cells = [
-                jnp.where(here, value, 0.0).astype(BF16)
-                for value in (
-                    (local & 127).astype(F32),
-                    lax.shift_right_logical(local, 7).astype(F32),
-                    tx_ref[s, 0:1, :],
-                    ty_ref[s, 0:1, :],
+            members, cells = [], []
+            for c in range(GROUP):
+                ids = ids_ref[s, pl.ds(k * GROUP + c, 1), :]
+                owner = lax.shift_right_logical(ids, 11)
+                member = row_iota == owner
+                member_bf = jnp.where(member, 1.0, 0.0).astype(BF16)
+                ahead = jnp.dot(member_bf, upper, preferred_element_type=F32)
+                rank = jnp.sum(
+                    jnp.where(member, ahead[:, :LANES] + counts, 0.0), axis=0, keepdims=True
+                ).astype(I32)
+                counts = counts + ahead[:, LANES:]
+                slot_ref[s, pl.ds(k * GROUP + c, 1), :] = owner * LANES + rank
+                here = row_iota == rank
+                low = (ids & 127).astype(F32)
+                high = (lax.shift_right_logical(ids, 7) & 15).astype(F32) * 16.0 + own_tile
+                members.append(member_bf)
+                cells.append(
+                    jnp.concatenate(
+                        [
+                            jnp.where(here, low, 0.0).astype(BF16),
+                            jnp.where(here, high, 0.0).astype(BF16),
+                        ],
+                        0,
+                    )
                 )
-            ]
             acc = acc + lax.dot_general(
-                member_bf,
-                jnp.concatenate(cells, 0),
+                jnp.concatenate(members, 1),
+                jnp.concatenate(cells, 1),
                 (((1,), (1,)), ((), ())),
                 preferred_element_type=F32,
             )
             out.append((counts, acc))
         return tuple(out)
 
-    start = tuple((zero, jnp.zeros((OWN, 4 * LANES), F32)) for _ in range(STEPS))
-    done = lax.fori_loop(0, SLABS, body, start, unroll=2)
+    start = tuple((zero, jnp.zeros((OWN, 2 * LANES), F32)) for _ in range(STEPS))
+    done = lax.fori_loop(0, SLABS // GROUP, body, start)
     for s in range(STEPS):
         acc = done[s][1].astype(I32)
-        want_ref[s] = acc[:, 0:128] + acc[:, 128:256] * 128
-        tile_ref[s] = acc[:, 256:384] + acc[:, 384:512] * IMG_TX
-
-
-def routing(ids, tile_x, tile_y):
+        high = acc[:, LANES:]
+        request[s] = acc[:, :LANES] + lax.shift_right_logical(high, 4) * 128
+        request[STEPS + s] = jnp.take_along_axis(
+            jnp.broadcast_to(tile_ref[s], (OWN, LANES)),
+            high & 15,
+            axis=1,
+            mode="promise_in_bounds",
+        )
+    all_entered()
+    me = my_index()
+
+    def push(k, _):
+        send(request, asked_ref, lax.rem(me + k, OWN), send_sem, recv_sem)
+        return 0
+
+    lax.fori_loop(1, OWN, push, 0, unroll=2)
+    keep_own(request, asked_ref)
+    rest = all_but_one(request, asked_ref, send_sem, recv_sem)
+    rest.wait_send()
+    rest.wait_recv()
+
+
+def routing(ids, lane_tiles):
     strict = np.triu(np.ones((128, 128), np.float32), 1)
     upper = jnp.asarray(np.concatenate([strict, np.ones((128, 128), np.float32)], 1), BF16)
+    vmem = pl.BlockSpec(memory_space=pltpu.VMEM)
     return pl.pallas_call(
         routing_kernel,
         out_shape=(
             jax.ShapeDtypeStruct((STEPS, SLABS, LANES), I32),
-            jax.ShapeDtypeStruct((STEPS, OWN, LANES), I32),
-            jax.ShapeDtypeStruct((STEPS, OWN, LANES), I32),
+            jax.ShapeDtypeStruct((2 * STEPS, OWN, LANES), I32),
         ),
-        compiler_params=params_of(32),
+        in_specs=[vmem] * 3,
+        out_specs=(vmem, vmem),
+        scratch_shapes=[
+            pltpu.VMEM((2 * STEPS, OWN, LANES), I32),
+            pltpu.SemaphoreType.DMA,
+            pltpu.SemaphoreType.DMA,
+        ],
+        compiler_params=remote_params(0),
         name="routing",
-    )(ids, tile_x, tile_y, upper)
-
-
-def gather_kernel(table_ref, want_ref, tile_ref, out_ref, shift_ref, parts, got):
+    )(ids, lane_tiles, upper)
+
+
+BLOCKS = 8
+
+
+def gather_kernel(
+    step, table_ref, asked_ref, out_ref, shift_ref, parts, got, answer, send_sem, recv_sem
+):
+    greet()
     for f in range(FIELDS):
         for p, part in enumerate(split3(table_ref[f])):
             parts[f * 16 : f * 16 + 16, p * 128 : p * 128 + 128] = part.astype(BF16)
     low_iota = lax.broadcasted_iota(I32, (128, 256), 0)
     high_iota = lax.broadcasted_iota(I32, (16, 256), 0)
-
-    def body(c, _):
-        want = jnp.concatenate(
-            [want_ref[pl.ds(2 * c, 1), :], want_ref[pl.ds(2 * c + 1, 1), :]], 1
-        )
-        hot = jnp.where(low_iota == (want & 127), 1.0, 0.0).astype(BF16)
-        hot = jnp.concatenate([hot, hot, hot], 0)
-        here = high_iota == lax.shift_right_logical(want, 7)
-        picked = jnp.dot(parts[...], hot, preferred_element_type=F32)
-        for f in range(FIELDS):
-            row = jnp.sum(
-                jnp.where(here, picked[f * 16 : f * 16 + 16], 0.0), axis=0, keepdims=True
+    me = my_index()
+    groups = OWN // BLOCKS
+
+    def group_of(k):
+        return lax.rem(me // BLOCKS + k, groups)
+
+    def compute(group):
+        first = pl.multiple_of(group * BLOCKS, BLOCKS)
+        for pair in range(BLOCKS // 2):
+            d = first + 2 * pair
+            want = jnp.concatenate(
+                [asked_ref[step, pl.ds(d, 1), :], asked_ref[step, pl.ds(d + 1, 1), :]], 1
             )
-            got[f, pl.ds(2 * c, 1), :] = row[:, :128]
-            got[f, pl.ds(2 * c + 1, 1), :] = row[:, 128:]
-        return 0
-
-    lax.fori_loop(0, OWN // 2, body, 0, unroll=2)
-    tile = tile_ref[...]
-    centre_x = ((tile & (IMG_TX - 1)) * SIDE + SIDE // 2).astype(F32)
-    centre_y = (lax.shift_right_logical(tile, 6) * SIDE + SIDE // 2).astype(F32)
-    local_u = got[0] - centre_x
-    local_v = got[1] - centre_y
-    shift_ref[0] = local_u
-    shift_ref[1] = local_v
-    alpha, beta, gamma = got[2], got[3], got[4]
-    out_ref[0] = alpha
-    out_ref[1] = beta
-    out_ref[2] = gamma
-    out_ref[3] = -(alpha * local_u + beta * local_v)
-    out_ref[4] = -gamma * local_v
-    for f in range(5, FIELDS):
-        out_ref[f] = got[f]
-
-
-def owner_gather(table, want, tile):
+            hot = jnp.where(low_iota == (want & 127), 1.0, 0.0).astype(BF16)
+            hot = jnp.concatenate([hot, hot, hot], 0)
+            here = high_iota == lax.shift_right_logical(want, 7)
+            picked = jnp.dot(parts[...], hot, preferred_element_type=F32)
+            for f in range(FIELDS):
+                row = jnp.sum(
+                    jnp.where(here, picked[f * 16 : f * 16 + 16], 0.0), axis=0, keepdims=True
+                )
+                got[f, 2 * pair : 2 * pair + 1, :] = row[:, :128]
+                got[f, 2 * pair + 1 : 2 * pair + 2, :] = row[:, 128:]
+        at = pl.ds(first, BLOCKS)
+        tile = asked_ref[STEPS + step, at, :]
+        centre_x = ((tile & (IMG_TX - 1)) * SIDE + SIDE // 2).astype(F32)
+        centre_y = (lax.shift_right_logical(tile, 6) * SIDE + SIDE // 2).astype(F32)
+        local_u = got[0] - centre_x
+        local_v = got[1] - centre_y
+        shift_ref[0, at, :] = local_u
+        shift_ref[1, at, :] = local_v
+        alpha, beta, gamma = got[2], got[3], got[4]
+        answer[0, at, :] = alpha
+        answer[1, at, :] = beta
+        answer[2, at, :] = gamma
+        answer[3, at, :] = -(alpha * local_u + beta * local_v)
+        answer[4, at, :] = -gamma * local_v
+        for f in range(5, FIELDS):
+            answer[f, at, :] = got[f]
+
+    def push(group):
+        def one(k, _):
+            peer = group * BLOCKS + lax.rem(me + k, BLOCKS)
+
+            @pl.when(peer != me)
+            def _():
+                send(answer, out_ref, peer, send_sem, recv_sem)
+
+            return 0
+
+        lax.fori_loop(0, BLOCKS, one, 0)
+
+    def early(k, _):
+        compute(group_of(k))
+        return 0
+
+    lax.fori_loop(0, groups // 2, early, 0)
+    all_entered()
+
+    def late(k, _):
+        push(group_of(k))
+        compute(group_of(k + groups // 2))
+        return 0
+
+    lax.fori_loop(0, groups // 2, late, 0)
+
+    def last(k, _):
+        push(group_of(k + groups // 2))
+        return 0
+
+    lax.fori_loop(0, groups // 2, last, 0)
+    keep_own(answer, out_ref)
+    rest = all_but_one(answer, out_ref, send_sem, recv_sem)
+    rest.wait_send()
+    rest.wait_recv()
+
+
+def owner_gather(step, table, asked):
+    vmem = pl.BlockSpec(memory_space=pltpu.VMEM)
     return pl.pallas_call(
-        gather_kernel,
+        functools.partial(gather_kernel, step),
         out_shape=(
             jax.ShapeDtypeStruct((FIELDS, OWN, LANES), F32),
             jax.ShapeDtypeStruct((2, OWN, LANES), F32),
         ),
+        in_specs=[vmem] * 2,
+        out_specs=(vmem, vmem),
         scratch_shapes=[
             pltpu.VMEM((FIELDS * 16, 384), BF16),
+            pltpu.VMEM((FIELDS, BLOCKS, LANES), F32),
             pltpu.VMEM((FIELDS, OWN, LANES), F32),
+            pltpu.SemaphoreType.DMA,
+            pltpu.SemaphoreType.DMA,
         ],
-        compiler_params=params_of(32),
+        compiler_params=remote_params(1 + step),
         name="owner_gather",
-    )(table, want, tile)
-
-
-def scatter_kernel(moment_ref, shift_ref, want_ref, out_ref, high, rest):
-    local_u, local_v = shift_ref[0], shift_ref[1]
-    m0, mx, my = moment_ref[0], moment_ref[1], moment_ref[2]
-    sx = mx - local_u * m0
-    sy = my - local_v * m0
-    sums = [
-        sx,
-        sy,
-        moment_ref[3] - local_u * (mx + sx),
-        moment_ref[4] - local_u * my - local_v * sx,
-        moment_ref[5] - local_v * (my + sy),
-        m0,
-        moment_ref[6],
-        moment_ref[7],
-        moment_ref[8],
-    ]
-    for f in range(FIELDS):
-        top = sums[f].astype(BF16).astype(F32)
-        high[f] = top
-        rest[f] = sums[f] - top
+    )(table, asked)
+
+
+def scatter_kernel(
+    step, moment_ref, shift_ref, asked_ref, out_ref, loss_ref,
+    arrived, high, rest, own_sem, send_sem, recv_sems,
+):
+    greet()
+    me = my_index()
+    groups = OWN // BLOCKS
+    mine = me // BLOCKS
+    all_entered()
+
+    def push(k, _):
+        send(moment_ref, arrived, lax.rem(me + k, OWN), send_sem, recv_sems.at[mine])
+        return 0
+
+    lax.fori_loop(1, OWN, push, 0, unroll=2)
+    own = pltpu.make_async_copy(moment_ref.at[:, me, :], arrived.at[:, me, :], own_sem)
+    own.start()
+    own.wait()
     low_iota = lax.broadcasted_iota(I32, (128, 128), 0)
     high_iota = lax.broadcasted_iota(I32, (16, 128), 0)
 
-    def body(c, acc):
-        lefts, rights = [], []
-        for half in range(2):
-            d = 2 * c + half
-            want = want_ref[pl.ds(d, 1), :]
-            rights.append(jnp.where(low_iota == (want & 127), 1.0, 0.0).astype(BF16))
-            here = high_iota == lax.shift_right_logical(want, 7)
-            rows = [
-                jnp.where(here, ref[f, pl.ds(d, 1), :], 0.0).astype(BF16)
-                for ref in (high, rest)
-                for f in range(FIELDS)
-            ]
-            lefts.append(jnp.concatenate(rows, 0))
-        return acc + lax.dot_general(
-            jnp.concatenate(lefts, 1),
-            jnp.concatenate(rights, 1),
-            (((1,), (1,)), ((), ())),
-            preferred_element_type=F32,
-        )
-
-    acc = lax.fori_loop(
-        0, OWN // 2, body, jnp.zeros((2 * FIELDS * 16, 128), F32), unroll=2
+    def landed(group, count):
+        blocks = pl.ds(group * BLOCKS, count)
+        pltpu.make_async_remote_copy(
+            src_ref=moment_ref.at[:, blocks, :],
+            dst_ref=arrived.at[:, blocks, :],
+            send_sem=send_sem,
+            recv_sem=recv_sems.at[group],
+            device_id=mesh_place(me),
+            device_id_type=pl.DeviceIdType.MESH,
+        ).wait_recv()
+
+    def body(k, carry):
+        acc, loss = carry
+        group = lax.rem(mine + groups - k, groups)
+
+        @pl.when(k == 0)
+        def _():
+            landed(group, BLOCKS - 1)
+
+        @pl.when(k != 0)
+        def _():
+            landed(group, BLOCKS)
+
+        first = pl.multiple_of(group * BLOCKS, BLOCKS)
+        at = pl.ds(first, BLOCKS)
+        local_u, local_v = shift_ref[0, at, :], shift_ref[1, at, :]
+        m0, mx, my = arrived[0, at, :], arrived[1, at, :], arrived[2, at, :]
+        sx = mx - local_u * m0
+        sy = my - local_v * m0
+        sums = [
+            sx,
+            sy,
+            arrived[3, at, :] - local_u * (mx + sx),
+            arrived[4, at, :] - local_u * my - local_v * sx,
+            arrived[5, at, :] - local_v * (my + sy),
+            m0,
+            arrived[6, at, :],
+            arrived[7, at, :],
+            arrived[8, at, :],
+        ]
+        for f in range(FIELDS):
+            top = sums[f].astype(BF16).astype(F32)
+            high[f] = top
+            rest[f] = sums[f] - top
+        for pair in range(BLOCKS // 2):
+            lefts, rights = [], []
+            for half in range(2):
+                d = 2 * pair + half
+                want = asked_ref[step, pl.ds(first + d, 1), :]
+                rights.append(jnp.where(low_iota == (want & 127), 1.0, 0.0).astype(BF16))
+                here = high_iota == lax.shift_right_logical(want, 7)
+                rows = [
+                    jnp.where(here, ref[f, d : d + 1, :], 0.0).astype(BF16)
+                    for ref in (high, rest)
+                    for f in range(FIELDS)
+                ]
+                lefts.append(jnp.concatenate(rows, 0))
+            acc = acc + lax.dot_general(
+                jnp.concatenate(lefts, 1),
+                jnp.concatenate(rights, 1),
+                (((1,), (1,)), ((), ())),
+                preferred_element_type=F32,
+            )
+        return acc, loss + arrived[FIELDS, at, :]
+
+    acc, loss = lax.fori_loop(
+        0,
+        groups,
+        body,
+        (jnp.zeros((2 * FIELDS * 16, 128), F32), jnp.zeros((BLOCKS, LANES), F32)),
     )
     out_ref[...] = acc[: FIELDS * 16] + acc[FIELDS * 16 :]
-
-
-def owner_scatter(moments, shifts, want):
+    loss_ref[...] = jnp.sum(loss, axis=0, keepdims=True)
+    all_but_one(moment_ref, arrived, send_sem, own_sem).wait_send()
+
+
+def owner_scatter(step, moments, shifts, asked):
+    vmem = pl.BlockSpec(memory_space=pltpu.VMEM)
     return pl.pallas_call(
-        scatter_kernel,
-        out_shape=jax.ShapeDtypeStruct((FIELDS * 16, 128), F32),
+        functools.partial(scatter_kernel, step),
+        out_shape=(
+            jax.ShapeDtypeStruct((FIELDS * 16, 128), F32),
+            jax.ShapeDtypeStruct((1, LANES), F32),
+        ),
+        in_specs=[vmem] * 3,
+        out_specs=(vmem, vmem),
         scratch_shapes=[
-            pltpu.VMEM((FIELDS, OWN, LANES), F32),
-            pltpu.VMEM((FIELDS, OWN, LANES), F32),
+            pltpu.VMEM((FIELDS + 1, OWN, LANES), F32),
+            pltpu.VMEM((FIELDS, BLOCKS, LANES), F32),
+            pltpu.VMEM((FIELDS, BLOCKS, LANES), F32),
+            pltpu.SemaphoreType.DMA,
+            pltpu.SemaphoreType.DMA,
+            pltpu.SemaphoreType.DMA((OWN // BLOCKS,)),
         ],
-        compiler_params=params_of(32),
+        compiler_params=remote_params(1 + STEPS + step),
         name="owner_scatter",
-    )(moments, shifts, want)
+    )(moments, shifts, asked)
 
 
 def render_constants():
@@ -333,8 +545,8 @@
 
 def render_kernel(
     slot_ref, fields_ref, target_ref, lines_ref, mono_ref,
-    picture_ref, moment_ref, loss_ref,
-    table, rows, line_a, line_b, alphas, weights, out_a, out_b, resid, back,
+    picture_ref, moment_ref,
+    table, rows, alphas, weights, out_a, out_b, resid, back,
 ):
     def build(o, _):
         first = fields_ref[0:8, pl.ds(o, 1), :].reshape(8, LANES)
@@ -351,24 +563,28 @@
 
     lax.fori_loop(0, OWN, zero_out, 0)
 
+    sublane = lax.broadcasted_iota(I32, (8, LANES), 0)
+
     def fetch(slab, i):
-        source = jnp.minimum(slab, SLABS - 1)
-        for t in range(TILES_DEV):
-            q = i * TILES_DEV + t
-            rows[pl.ds(pl.multiple_of(slab * 128, 128) + q, 1), :] = table[
-                pl.ds(slot_ref[source * 128 + q], 1), :
-            ]
-
-    def lines_of(slab, line):
-        left = rows[pl.ds(pl.multiple_of(slab * 128, 128), 128), 0:32].astype(BF16)
-        line[...] = jnp.dot(left, lines_ref[...], preferred_element_type=F32)
-
-    def forward(slab, line, state):
+        source = jnp.minimum(slab, SLABS - 1) * 128 + i * TILES_DEV
+        for half in range(0, TILES_DEV, 8):
+            got = None
+            for t in range(8):
+                row = table[pl.ds(slot_ref[source + half + t], 1), :]
+                row = jnp.broadcast_to(row, (8, LANES))
+                got = row if t == 0 else jnp.where(sublane == t, row, got)
+            at = pl.multiple_of(slab * 128, 128) + i * TILES_DEV + half
+            rows[pl.ds(at, 8), :] = got
+
+    def forward(slab, state):
         through, red, green, blue = state
         for i in range(8):
             at = pl.ds(pl.multiple_of(slab * 128, 128) + i * 16, 16)
-            first = line[i * 16 : i * 16 + 16, 0:256]
-            second = line[i * 16 : i * 16 + 16, 256:512]
+            both = jnp.dot(
+                rows[at, 0:32].astype(BF16), lines_ref[...], preferred_element_type=F32
+            )
+            first = both[:, 0:256]
+            second = both[:, 256:512]
             cols = rows[at, COL_OPACITY : COL_OPACITY + 4]
             alpha = jnp.exp2(cols[:, 0:1] - first * first - second * second)
             weight = through * alpha
@@ -378,23 +594,18 @@
             blue = blue + weight * cols[:, 3:4]
             alphas[at, :] = alpha
             weights[at, :] = weight
-            fetch(slab + 2, i)
+            fetch(slab + 1, i)
         return through, red, green, blue
 
-    for slab in range(2):
-        for i in range(8):
-            fetch(slab, i)
-    lines_of(0, line_a)
-
-    def forward_pair(pair, state):
-        lines_of(2 * pair + 1, line_b)
-        state = forward(2 * pair, line_a, state)
-        lines_of(2 * pair + 2, line_a)
-        return forward(2 * pair + 1, line_b, state)
-
+    for i in range(8):
+        fetch(0, i)
     blank = jnp.zeros((TILES_DEV, PIX), F32)
     _, red, green, blue = lax.fori_loop(
-        0, SLABS // 2, forward_pair, (jnp.ones((TILES_DEV, PIX), F32), blank, blank, blank)
+        0,
+        SLABS,
+        forward,
+        (jnp.ones((TILES_DEV, PIX), F32), blank, blank, blank),
+        unroll=4,
     )
     residuals = []
     total = jnp.zeros((), F32)
@@ -403,7 +614,7 @@
         residual = colour - target_ref[ch]
         residuals.append(residual)
         total = total + jnp.sum(residual * residual)
-    loss_ref[...] = jnp.full((1, LANES), 0.5 * total, F32)
+    moment_ref[FIELDS] = jnp.full((OWN, LANES), 0.5 * total, F32)
     res_red, res_green, res_blue = residuals
 
     padded = jnp.concatenate([jnp.zeros((16, PIX), F32), *residuals, jnp.zeros((64, PIX), F32)], 0)
@@ -455,7 +666,7 @@
         behind = backward(slab, behind, out_b, slab + 1, out_a)
         return backward(slab - 1, behind, out_a, slab, out_b)
 
-    behind = lax.fori_loop(0, SLABS // 2 - 1, backward_pair, behind)
+    behind = lax.fori_loop(0, SLABS // 2 - 1, backward_pair, behind, unroll=2)
     backward(0, behind, out_b, 1, out_a)
     for i in range(8):
         scatter(0, i, out_b)
@@ -480,16 +691,13 @@
         render_kernel,
         out_shape=(
             jax.ShapeDtypeStruct((3, TILES_DEV, PIX), F32),
-            jax.ShapeDtypeStruct((FIELDS, OWN, LANES), F32),
-            jax.ShapeDtypeStruct((1, LANES), F32),
+            jax.ShapeDtypeStruct((FIELDS + 1, OWN, LANES), F32),
         ),
         in_specs=[pl.BlockSpec(memory_space=pltpu.SMEM)] + [vmem] * 4,
-        out_specs=(vmem, vmem, vmem),
+        out_specs=(vmem, vmem),
         scratch_shapes=[
             pltpu.VMEM((OWN * LANES, LANES), F32),
             pltpu.VMEM((entries + 256, LANES), F32),
-            pltpu.VMEM((128, 512), F32),
-            pltpu.VMEM((128, 512), F32),
             pltpu.VMEM((entries, PIX), F32),
             pltpu.VMEM((entries, PIX), F32),
             pltpu.VMEM((128, LANES), F32),
@@ -502,10 +710,6 @@
     )(slots, fields, target, lines, mono)
 
 
-def exchange(blocks):
-    return lax.all_to_all(blocks, ("gx", "gy"), split_axis=1, concat_axis=1, tiled=True)
-
-
 def adam_update(params, moment_one, second, gradient, step_index):
     step_count = adam_start + step_index + 1
     moment_one = beta_one * moment_one + (1.0 - beta_one) * gradient
@@ -521,27 +725,21 @@
     params, moment_one, moment_two = (gauss_params, first_moment, second_moment)
     ids = jnp.swapaxes(splat_lists, 1, 2).reshape(STEPS, SLABS, LANES)
     lane_tiles = jnp.tile(tile_ids, (1, LANES // TILES_DEV))
-    tile_x = (lane_tiles % IMG_TX).astype(F32)[:, None, :]
-    tile_y = (lane_tiles // IMG_TX).astype(F32)[:, None, :]
-    slots, want, tiles = routing(ids, tile_x, tile_y)
+    slots, asked = routing(ids, lane_tiles[:, None, :])
     slots = slots.reshape(STEPS, SLABS * LANES)
-    asked = exchange(jnp.concatenate([want, tiles], 0))
     pictures = []
     losses = []
     for step_index in range(STEPS):
-        wanted, wanted_tile = asked[step_index], asked[STEPS + step_index]
         projected, pullback, inverses = jax.vjp(
             lambda values: project(values, camera[step_index]), params, has_aux=True
         )
         table = factor_rows(projected, inverses).reshape(FIELDS, 16, 128)
-        fields, shifts = owner_gather(table, wanted, wanted_tile)
-        fields = exchange(fields)
+        fields, shifts = owner_gather(step_index, table, asked)
         target = jnp.swapaxes(targets[step_index], 0, 1)
-        picture, moments, loss = render(slots[step_index], fields, target)
-        extra = jnp.broadcast_to(loss[None], (1, OWN, LANES))
-        arrived = exchange(jnp.concatenate([moments, extra], 0))
-        losses.append(jnp.sum(arrived[FIELDS, :, 0]))
-        sums = owner_scatter(arrived, shifts, wanted).reshape(FIELDS, local_count)
+        picture, moments = render(slots[step_index], fields, target)
+        sums, loss = owner_scatter(step_index, moments, shifts, asked)
+        sums = sums.reshape(FIELDS, local_count)
+        losses.append(loss[0, 0])
         conic_a, conic_b, conic_c = projected[2], projected[3], projected[4]
         cotangent = jnp.concatenate(
             [

time: 298 us -> 209 us (0.70)
  blocking collectives: 46.6 us -> 0 us
  waiting for transfers between devices: 42.1 us -> 0 us
  Pallas kernels: 154 us -> 183 us
  starting transfers between devices: 20.6 us -> 0 us
  local copies, waits for them, and re-layouts: 14.9 us -> 9.65 us
    all_to_all x2 -> x0, blocking collectives: 46.6 us -> none  [exchange(): lax.all_to_all(blocks, ('gx', 'gy'), split_axis=1, concat_axis=1, tiled=T...]
    pallas_call x4, Pallas kernels: 32.6 us -> 78.6 us  [the longest x2 43.6 us: owner_scatter(): pl.pallas_call(functools.partial(scatter_kernel, step), out_shape=(jax.Sh...]
    all_to_all x3 -> x0, waiting for transfers between devices: 42.1 us -> none  [exchange(): lax.all_to_all(blocks, ('gx', 'gy'), split_axis=1, concat_axis=1, tiled=T...]
    all_to_all x3 -> x0, starting transfers between devices: 20.6 us -> none  [exchange(): lax.all_to_all(blocks, ('gx', 'gy'), split_axis=1, concat_axis=1, tiled=T...]
    pallas_call x1, Pallas kernels: 37 us -> 28 us  [routing(): pl.pallas_call(routing_kernel, out_shape=(jax.ShapeDtypeStruct((STEPS, SL...]
    pallas_call x2, Pallas kernels: 84 us -> 76.2 us  [render(): pl.pallas_call(render_kernel, out_shape=(jax.ShapeDtypeStruct((3, TILES_D...]
    unnamed x42 -> x38, local copies, waits for them, and re-layouts: 3.5 us -> 6.7 us
  transfers between devices with their start and end apart: 3 -> 0, of which waited for: 3 -> 0; matrix products, arithmetic and copies ran while one was open for 2% -> 0% of each run, Pallas kernels for 0% -> 0%
where the time goes in v2:
time: 209 us
  Pallas kernels  183 us (88%)
  other arithmetic  15.3 us (7%)
  local copies, waits for them, and re-layouts  9.65 us (5%)
    pallas_call x2, Pallas kernels, render(): pl.pallas_call(render_kernel, out_shape=(jax.ShapeDtypeStruct((3, TILES_D...  76.2 us
    pallas_call x2, Pallas kernels, owner_scatter(): pl.pallas_call(functools.partial(scatter_kernel, step), out_shape=(jax.Sh...  43.6 us
    pallas_call x2, Pallas kernels, owner_gather(): pl.pallas_call(functools.partial(gather_kernel, step), out_shape=(jax.Sha...  35 us
    pallas_call x1, Pallas kernels, routing(): pl.pallas_call(routing_kernel, out_shape=(jax.ShapeDtypeStruct((STEPS, SL...  28 us
    unnamed x38, local copies, waits for them, and re-layouts  6.7 us
    select_n x2, other arithmetic, factor_rows(): beta = jnp.where(has_a, half_log2e * conic_b / root, 0.0)  4.36 us

profile of v2, /device:TPU:1, one launch (start us, length us, event | category | flops | bytes accessed | tf_op | source)
XLA Modules:
  0.0 208.9 jit_solution(4264519800709291645)
XLA Ops:
  0.6 0.7 copy-done.12
  1.3 0.7 fusion.81
  2.0 0.7 copy-done.13
  2.7 0.1 tile.9.tile_ref
  2.7 1.3 select_multiply_fusion.1
  4.1 0.0 copy-start.8
  4.1 2.8 %multiply_select_fusion.2 = (f32[1,2048]{1,0:T(1,128)S(1)}, f32[1,2048]{1,0:T(1,128)S(1)}, f32[1,2048]{1,0:T(1,128)S(1)}, f32[1,2048]{1,0:T(1,128)S(1)}, f32[1,2...) fusion(f32[1,2048]{1,0:T(1,128)S(1)} %get-tuple-element.83, ...), kind=kLoop, calls=%fused_computation.162 | loop fusion | flops 63488 | bytes 147464 | tf_op jit(solution)/shard_map/jit(_where)/select_n | solution.py:115
  7.0 0.6 slice_bitcast_fusion
  7.6 0.1 multiply_multiply_fusion.18
  7.7 0.2 stack.12
  8.0 0.1 multiply_reduce_fusion.3
  8.1 0.8 copy-done.9
  8.9 0.2 copy.18
  9.1 0.0 copy-start.4
  9.1 0.2 reshape.208.ids_ref
  9.3 0.6 copy-done.4
  10.0 28.0 %routing.1 = (s32[2,64,128]{2,1,0:T(8,128)S(1)}, s32[4,128,128]{2,1,0:T(8,128)S(1)}) custom-call(s32[2,64,128]{2,1,0:T(8,128)S(1)} %reshape.208.ids_ref, s32[2,1,128]{2,1,0:T(1,128)S(1)} %tile.9.tile_ref, bf16[128,256]{1,0:T(8,128)(2,1)S(1)} %copy-done.4), custom_call_target="tpu_custom_call" | custom-call | tf_op jit(solution)/shard_map/routing/pallas_call | solution.py:275
  38.0 0.6 slice_bitcast_fusion.2
  38.6 17.4 %owner_gather.2 = (f32[9,128,128]{2,1,0:T(8,128)S(1)}, f32[2,128,128]{2,1,0:T(8,128)S(1)}) custom-call(f32[9,16,128]{2,1,0:T(8,128)S(1)} %constant_dynamic-update-slice_fusion.table_ref, s32[4,128,128]{2,1,0:T(8,128)S(1)} %get-tuple-element.25.asked_ref), custom_call_target="tpu_custom_call" | custom-call | tf_op jit(solution)/shard_map/owner_gather/pallas_call | solution.py:384
  56.1 0.8 copy-done.3
  56.9 38.1 %render.2 = (f32[3,16,256]{2,1,0:T(8,128)}, f32[10,128,128]{2,1,0:T(8,128)}) custom-call(s32[8192]{0:T(1024)} %get-tuple-element.127.slot_ref, f32[9,128,128]{2,1,0:T(8,128)} %copy-done.3, f32[3,16,256]{2,1,0:T(8,128)} %get-tuple-element.115.target_ref, bf16[32,512]{1,0:T(8,128)(2,1)} %constant.104.clone.lines_ref, bf16[256,128]{1,0:T(8,128)(2,1)} %constant.105.clone.mono_ref), custom_call_target="tpu_custom_call" | custom-call | tf_op jit(solution)/shard_map/render/pallas_call | solution.py:690
  95.0 1.1 copy-done.1
  96.1 21.8 %owner_scatter.2 = (f32[144,128]{1,0:T(8,128)S(1)}, f32[1,128]{1,0:T(1,128)S(1)}) custom-call(f32[10,128,128]{2,1,0:T(8,128)S(1)} %copy-done.1, f32[2,128,128]{2,1,0:T(8,128)S(1)} %get-tuple-element.28.shift_ref, s32[4,128,128]{2,1,0:T(8,128)S(1)} %get-tuple-element.25.asked_ref), custom_call_target="tpu_custom_call" | custom-call | tf_op jit(solution)/shard_map/owner_scatter/pallas_call | solution.py:503
  118.0 0.1 broadcast_multiply_fusion.1
  118.0 0.0 copy-start.6
  118.1 0.6 slice_divide_fusion.3
  118.7 0.3 slice_divide_fusion.2
  119.0 0.4 fusion.2
  119.4 1.4 fusion.12
  120.8 0.5 divide_subtract_fusion.1
  121.3 0.3 select_multiply_fusion
  121.6 1.6 multiply_select_fusion
  123.3 0.1 multiply_multiply_fusion.9
  123.4 0.2 stack.13
  123.7 0.1 multiply_reduce_fusion.1
  123.8 17.6 %owner_gather.3 = (f32[9,128,128]{2,1,0:T(8,128)S(1)}, f32[2,128,128]{2,1,0:T(8,128)S(1)}) custom-call(f32[9,16,128]{2,1,0:T(8,128)S(1)} %constant_dynamic-update-slice_fusion.7.table_ref, s32[4,128,128]{2,1,0:T(8,128)S(1)} %get-tuple-element.25.asked_ref), custom_call_target="tpu_custom_call" | custom-call | tf_op jit(solution)/shard_map/owner_gather/pallas_call | solution.py:384
  141.4 0.8 copy-done.2
  142.2 38.1 %render.3 = (f32[3,16,256]{2,1,0:T(8,128)}, f32[10,128,128]{2,1,0:T(8,128)}) custom-call(s32[8192]{0:T(1024)} %get-tuple-element.126.slot_ref, f32[9,128,128]{2,1,0:T(8,128)} %copy-done.2, f32[3,16,256]{2,1,0:T(8,128)} %get-tuple-element.114.target_ref, bf16[32,512]{1,0:T(8,128)(2,1)} %constant.104.clone.lines_ref, bf16[256,128]{1,0:T(8,128)(2,1)} %constant.105.clone.mono_ref), custom_call_target="tpu_custom_call" | custom-call | tf_op jit(solution)/shard_map/render/pallas_call | solution.py:690
  180.3 1.1 copy-done
  181.4 21.8 %owner_scatter.3 = (f32[144,128]{1,0:T(8,128)S(1)}, f32[1,128]{1,0:T(1,128)S(1)}) custom-call(f32[10,128,128]{2,1,0:T(8,128)S(1)} %copy-done, f32[2,128,128]{2,1,0:T(8,128)S(1)} %get-tuple-element.34.shift_ref, s32[4,128,128]{2,1,0:T(8,128)S(1)} %get-tuple-element.25.asked_ref), custom_call_target="tpu_custom_call" | custom-call | tf_op jit(solution)/shard_map/owner_scatter/pallas_call | solution.py:503
  203.2 0.6 maximum_multiply_fusion
  203.9 0.7 pad_maximum_fusion
  204.5 0.1 broadcast_multiply_fusion
  204.6 0.6 slice_divide_fusion.1
  205.2 0.3 slice_divide_fusion
  205.5 0.4 fusion.13
  205.9 1.3 fusion.23
  207.2 1.6 divide_subtract_fusion
  (45 shorter events, 0.3 us)
Async XLA Ops:
  0.6 0.7 copy-start.12
  2.0 0.7 copy-start.13
  4.1 2.9 %copy-start.8 = (f32[2,16,3,256]{3,1,2,0:T(8,128)S(1)}, f32[2,16,3,256]{3,1,2,0:T(8,128)}, u32[]{:S(2)}) copy-start(f32[2,16,3,256]{3,1,2,0:T(8,128)} %param.18) | copy-start | bytes 294916
  4.1 3.9 %copy-start.5 = (f32[55,2048]{1,0:T(8,128)S(1)}, f32[55,2048]{1,0:T(8,128)}, u32[]{:S(2)}) copy-start(f32[55,2048]{1,0:T(8,128)} %param.13) | copy-start | bytes 1351684
  8.1 0.8 copy-start.9
  9.1 0.8 copy-start.4
  56.0 0.8 copy-start.3
  95.0 1.1 copy-start.1
  118.0 2.8 %copy-start.7 = (f32[55,2048]{1,0:T(8,128)S(1)}, f32[55,2048]{1,0:T(8,128)}, u32[]{:S(2)}) copy-start(f32[55,2048]{1,0:T(8,128)} %param.15) | copy-start | bytes 1351684
  118.0 2.7 %copy-start.6 = (f32[55,2048]{1,0:T(8,128)S(1)}, f32[55,2048]{1,0:T(8,128)}, u32[]{:S(2)}) copy-start(f32[55,2048]{1,0:T(8,128)} %param.14) | copy-start | bytes 1351684
  141.4 0.8 copy-start.2
  180.3 1.1 copy-start
  181.4 22.4 %copy-start.10 = (f32[3,16,256]{2,1,0:T(8,128)S(1)}, f32[3,16,256]{2,1,0:T(8,128)}, u32[]{:S(2)}) copy-start(f32[3,16,256]{2,1,0:T(8,128)} %get-tuple-element.37) | copy-start | bytes 147460
  181.4 22.5 %copy-start.11 = (f32[3,16,256]{2,1,0:T(8,128)S(1)}, f32[3,16,256]{2,1,0:T(8,128)}, u32[]{:S(2)}) copy-start(f32[3,16,256]{2,1,0:T(8,128)} %get-tuple-element.38) | copy-start | bytes 147460

commit v3 on v2

--- a/solution.py
+++ b/solution.py
@@ -343,36 +343,36 @@
             answer[f, at, :] = got[f]
 
     def push(group):
-        def one(k, _):
+        for k in range(BLOCKS):
             peer = group * BLOCKS + lax.rem(me + k, BLOCKS)
-
-            @pl.when(peer != me)
-            def _():
-                send(answer, out_ref, peer, send_sem, recv_sem)
-
-            return 0
-
-        lax.fori_loop(0, BLOCKS, one, 0)
+            send(answer, out_ref, peer, send_sem, recv_sem)
 
     def early(k, _):
         compute(group_of(k))
         return 0
 
-    lax.fori_loop(0, groups // 2, early, 0)
+    half = groups // 2
+    lax.fori_loop(0, half, early, 0)
     all_entered()
 
     def late(k, _):
-        push(group_of(k))
-        compute(group_of(k + groups // 2))
+        push(group_of(2 * k + 1))
+        push(group_of(2 * k + 2))
+        compute(group_of(k + half))
         return 0
 
-    lax.fori_loop(0, groups // 2, late, 0)
-
-    def last(k, _):
-        push(group_of(k + groups // 2))
+    lax.fori_loop(0, half - 2, late, 0)
+    compute(group_of(groups - 2))
+    push(group_of(groups - 3))
+    compute(group_of(groups - 1))
+    push(group_of(groups - 2))
+    push(group_of(groups - 1))
+
+    def inside(k, _):
+        send(answer, out_ref, me // BLOCKS * BLOCKS + lax.rem(me + k, BLOCKS), send_sem, recv_sem)
         return 0
 
-    lax.fori_loop(0, groups // 2, last, 0)
+    lax.fori_loop(1, BLOCKS, inside, 0)
     keep_own(answer, out_ref)
     rest = all_but_one(answer, out_ref, send_sem, recv_sem)
     rest.wait_send()
@@ -521,6 +521,9 @@
     )(moments, shifts, asked)
 
 
+PACK = 8
+
+
 def render_constants():
     axis = np.arange(SIDE, dtype=np.float32) - 7.5
     x = np.tile(axis, SIDE)
@@ -534,19 +537,30 @@
     block[3] = np.concatenate([one, zero])
     block[4] = np.concatenate([zero, one])
     lines = np.concatenate([block, block, block, np.zeros_like(block)], 0)
-    mono = np.zeros((PIX, 128), np.float32)
+    mono = np.zeros((2 * PIX, 128), np.float32)
     for k, column in enumerate((one, x, y, x * x, x * y, y * y)):
-        mono[:, k] = column
-    return jnp.asarray(lines, BF16), jnp.asarray(mono, BF16)
-
-
+        mono[:, k * PACK : (k + 1) * PACK] = np.tile(column, 2)[:, None]
+    fold = np.zeros((256, 128), np.float32)
+    for ch in range(3):
+        for half in range(2):
+            at = half * 128 + ch * TILES_DEV
+            fold[at : at + TILES_DEV, (6 + ch) * PACK : (7 + ch) * PACK] = 1.0
+    return jnp.asarray(lines, BF16), jnp.asarray(mono, BF16), jnp.asarray(fold, BF16)
+
+
+BATCH = 2
 COL_OPACITY = 29
 
 
+def split2(values):
+    high = values.astype(BF16)
+    return high, (values - high.astype(F32)).astype(BF16)
+
+
 def render_kernel(
-    slot_ref, fields_ref, target_ref, lines_ref, mono_ref,
+    slot_ref, fields_ref, target_ref, lines_ref, mono_ref, fold_ref,
     picture_ref, moment_ref,
-    table, rows, alphas, weights, out_a, out_b, resid, back,
+    table, rows, alphas, weights, out_ref, resid, back,
 ):
     def build(o, _):
         first = fields_ref[0:8, pl.ds(o, 1), :].reshape(8, LANES)
@@ -556,12 +570,6 @@
         return 0
 
     lax.fori_loop(0, OWN, build, 0, unroll=4)
-
-    def zero_out(o, _):
-        back[pl.ds(pl.multiple_of(o * 128, 128), 128), :] = jnp.zeros((128, LANES), F32)
-        return 0
-
-    lax.fori_loop(0, OWN, zero_out, 0)
 
     sublane = lax.broadcasted_iota(I32, (8, LANES), 0)
 
@@ -594,6 +602,9 @@
             blue = blue + weight * cols[:, 3:4]
             alphas[at, :] = alpha
             weights[at, :] = weight
+            back[pl.ds(pl.multiple_of(slab * 256, 256) + i * 32, 32), :] = jnp.zeros(
+                (32, LANES), F32
+            )
             fetch(slab + 1, i)
         return through, red, green, blue
 
@@ -617,7 +628,7 @@
     moment_ref[FIELDS] = jnp.full((OWN, LANES), 0.5 * total, F32)
     res_red, res_green, res_blue = residuals
 
-    padded = jnp.concatenate([jnp.zeros((16, PIX), F32), *residuals, jnp.zeros((64, PIX), F32)], 0)
+    padded = jnp.concatenate([*residuals, jnp.zeros((80, PIX), F32)], 0)
     turned = padded.T
     top = turned.astype(BF16)
     resid[:, 0:128] = top
@@ -627,64 +638,65 @@
     row = lax.broadcasted_iota(I32, (128, LANES), 0)
     own_tile = (lane & 15) == (row & 15)
 
-    def scatter(slab, i, source):
+    def scatter(slab, i, source, base):
         for t in range(TILES_DEV):
             q = i * TILES_DEV + t
-            back[pl.ds(slot_ref[slab * 128 + q], 1), :] = source[q : q + 1, :]
-
-    def backward(slab, behind, target, previous, source):
-        pieces = [None] * 8
-        for i in range(7, -1, -1):
-            at = pl.ds(pl.multiple_of(slab * 128, 128) + i * 16, 16)
+            back[pl.ds(slot_ref[slab * 128 + q], 1), :] = source[base + q : base + q + 1, :]
+
+    own_rows = jnp.concatenate([own_tile] * BATCH, 0)
+
+    def backward(turn, behind, target, previous, source):
+        first = pl.multiple_of(turn * (BATCH * 128), BATCH * 128)
+        every = pl.ds(first, BATCH * 128)
+        weight_top, weight_rest = split2(weights[every, :])
+        both = jnp.dot(weight_top, resid[...], preferred_element_type=F32)
+        shade = both[:, :128] + both[:, 128:]
+        shade = shade + jnp.dot(weight_rest, resid[:, 0:128], preferred_element_type=F32)
+        shade = jnp.concatenate(split2(jnp.where(own_rows, shade, 0.0)), 1)
+        pieces = [None] * (8 * BATCH)
+        for i in range(8 * BATCH - 1, -1, -1):
+            at = pl.ds(first + i * 16, 16)
             cols = rows[at, COL_OPACITY : COL_OPACITY + 4]
-            alpha = alphas[at, :]
             gain = (
                 res_red * cols[:, 1:2] + res_green * cols[:, 2:3] + res_blue * cols[:, 3:4]
             ) - behind
             pieces[i] = weights[at, :] * gain
-            behind = behind + alpha * gain
+            behind = behind + alphas[at, :] * gain
             if source is not None:
-                scatter(previous, i, source)
-        slope = jnp.concatenate(pieces, 0)
-        slope_top = slope.astype(BF16)
-        slope_rest = (slope - slope_top.astype(F32)).astype(BF16)
-        weight = weights[pl.ds(pl.multiple_of(slab * 128, 128), 128), :]
-        weight_top = weight.astype(BF16)
-        weight_rest = (weight - weight_top.astype(F32)).astype(BF16)
-        moment = jnp.dot(slope_top, mono_ref[...], preferred_element_type=F32)
-        moment = moment + jnp.dot(slope_rest, mono_ref[...], preferred_element_type=F32)
-        both = jnp.dot(weight_top, resid[...], preferred_element_type=F32)
-        shade = both[:, :128] + both[:, 128:]
-        shade = shade + jnp.dot(weight_rest, resid[:, 0:128], preferred_element_type=F32)
-        target[...] = moment + jnp.where(own_tile, shade, 0.0)
+                scatter(previous * BATCH + i // 8, i % 8, source, i // 8 * 128)
+        slope = jnp.concatenate(split2(jnp.concatenate(pieces, 0)), 1)
+        target[...] = jnp.dot(slope, mono_ref[...], preferred_element_type=F32) + jnp.dot(
+            shade, fold_ref[...], preferred_element_type=F32
+        )
         return behind
 
-    behind = backward(SLABS - 1, blank, out_a, None, None)
-
-    def backward_pair(pair, behind):
-        slab = SLABS - 2 - 2 * pair
-        behind = backward(slab, behind, out_b, slab + 1, out_a)
-        return backward(slab - 1, behind, out_a, slab, out_b)
-
-    behind = lax.fori_loop(0, SLABS // 2 - 1, backward_pair, behind, unroll=2)
-    backward(0, behind, out_b, 1, out_a)
-    for i in range(8):
-        scatter(0, i, out_b)
-
-    def finish(o, _):
-        turned = back[pl.ds(pl.multiple_of(o * 128, 128), 128), 0:64].T
-        for k in range(6):
-            moment_ref[k, pl.ds(o, 1), :] = turned[k : k + 1]
-        for ch in range(3):
-            part = turned[16 + 16 * ch : 32 + 16 * ch]
-            moment_ref[6 + ch, pl.ds(o, 1), :] = jnp.sum(part, axis=0, keepdims=True)
-        return 0
-
-    lax.fori_loop(0, OWN, finish, 0, unroll=4)
+    batches = SLABS // BATCH
+    outs = [out_ref.at[k] for k in range(2)]
+    behind = backward(batches - 1, blank, outs[1], None, None)
+
+    def backward_two(k, behind):
+        turn = batches - 2 - 2 * k
+        behind = backward(turn, behind, outs[0], turn + 1, outs[1])
+        return backward(turn - 1, behind, outs[1], turn, outs[0])
+
+    behind = lax.fori_loop(0, batches // 2 - 1, backward_two, behind)
+    backward(0, behind, outs[0], 1, outs[1])
+    for i in range(8 * BATCH):
+        scatter(i // 8, i % 8, outs[0], i // 8 * 128)
+
+    turn = lax.broadcasted_iota(I32, (128, LANES), 1) & (PACK - 1)
+    for g in range(OWN // PACK):
+        merged = back[g * 1024 : g * 1024 + 128, :]
+        for k in range(1, PACK):
+            at = g * 1024 + k * 128
+            merged = jnp.where(turn == k, back[at : at + 128, :], merged)
+        merged = merged.T
+        for f in range(FIELDS):
+            moment_ref[f, g * PACK : (g + 1) * PACK, :] = merged[f * PACK : (f + 1) * PACK]
 
 
 def render(slots, fields, target):
-    lines, mono = render_constants()
+    constants = render_constants()
     vmem = pl.BlockSpec(memory_space=pltpu.VMEM)
     entries = SLABS * 128
     return pl.pallas_call(
@@ -693,21 +705,20 @@
             jax.ShapeDtypeStruct((3, TILES_DEV, PIX), F32),
             jax.ShapeDtypeStruct((FIELDS + 1, OWN, LANES), F32),
         ),
-        in_specs=[pl.BlockSpec(memory_space=pltpu.SMEM)] + [vmem] * 4,
+        in_specs=[pl.BlockSpec(memory_space=pltpu.SMEM)] + [vmem] * 5,
         out_specs=(vmem, vmem),
         scratch_shapes=[
             pltpu.VMEM((OWN * LANES, LANES), F32),
             pltpu.VMEM((entries + 256, LANES), F32),
             pltpu.VMEM((entries, PIX), F32),
             pltpu.VMEM((entries, PIX), F32),
-            pltpu.VMEM((128, LANES), F32),
-            pltpu.VMEM((128, LANES), F32),
+            pltpu.VMEM((2, BATCH * 128, LANES), F32),
             pltpu.VMEM((PIX, 256), BF16),
             pltpu.VMEM((OWN * LANES, LANES), F32),
         ],
         compiler_params=params_of(56),
         name="render",
-    )(slots, fields, target, lines, mono)
+    )(slots, fields, target, *constants)
 
 
 def adam_update(params, moment_one, second, gradient, step_index):

time: 209 us -> 199 us (0.952)
  Pallas kernels: 183 us -> 173 us
    pallas_call x2, Pallas kernels: 76.2 us -> 70.1 us  [render(): pl.pallas_call(render_kernel, out_shape=(jax.ShapeDtypeStruct((3, TILES_D...]
    pallas_call x2, Pallas kernels: 43.6 us -> 41.1 us  [owner_scatter(): pl.pallas_call(functools.partial(scatter_kernel, step), out_shape=(jax.Sh...]
where the time goes in v3:
time: 199 us
  Pallas kernels  173 us (87%)
  other arithmetic  15.3 us (8%)
  local copies, waits for them, and re-layouts  9.65 us (5%)
    pallas_call x2, Pallas kernels, render(): pl.pallas_call(render_kernel, out_shape=(jax.ShapeDtypeStruct((3, TILES_D...  70.1 us
    pallas_call x2, Pallas kernels, owner_scatter(): pl.pallas_call(functools.partial(scatter_kernel, step), out_shape=(jax.Sh...  41.1 us
    pallas_call x2, Pallas kernels, owner_gather(): pl.pallas_call(functools.partial(gather_kernel, step), out_shape=(jax.Sha...  33.6 us
    pallas_call x1, Pallas kernels, routing(): pl.pallas_call(routing_kernel, out_shape=(jax.ShapeDtypeStruct((STEPS, SL...  28 us
    unnamed x38, local copies, waits for them, and re-layouts  6.7 us
    select_n x2, other arithmetic, factor_rows(): beta = jnp.where(has_a, half_log2e * conic_b / root, 0.0)  4.36 us

profile of v3, /device:TPU:1, one launch (start us, length us, event | category | flops | bytes accessed | tf_op | source)
XLA Modules:
  0.0 198.9 jit_solution(2669058721386648522)
XLA Ops:
  0.6 0.7 copy-done.12
  1.3 0.7 fusion.81
  2.0 0.7 copy-done.13
  2.7 0.1 tile.9.tile_ref
  2.7 1.3 select_multiply_fusion.1
  4.1 0.0 copy-start.8
  4.1 2.8 %multiply_select_fusion.2 = (f32[1,2048]{1,0:T(1,128)S(1)}, f32[1,2048]{1,0:T(1,128)S(1)}, f32[1,2048]{1,0:T(1,128)S(1)}, f32[1,2048]{1,0:T(1,128)S(1)}, f32[1,2...) fusion(f32[1,2048]{1,0:T(1,128)S(1)} %get-tuple-element.83, ...), kind=kLoop, calls=%fused_computation.162 | loop fusion | flops 63488 | bytes 147464 | tf_op jit(solution)/shard_map/jit(_where)/select_n | solution.py:115
  7.0 0.6 slice_bitcast_fusion
  7.6 0.1 multiply_multiply_fusion.18
  7.7 0.2 stack.12
  8.0 0.1 multiply_reduce_fusion.3
  8.1 0.8 copy-done.9
  8.9 0.2 copy.20
  9.1 0.0 copy-start.4
  9.1 0.2 reshape.208.ids_ref
  9.3 0.6 copy-done.4
  10.0 28.0 %routing.1 = (s32[2,64,128]{2,1,0:T(8,128)S(1)}, s32[4,128,128]{2,1,0:T(8,128)S(1)}) custom-call(s32[2,64,128]{2,1,0:T(8,128)S(1)} %reshape.208.ids_ref, s32[2,1,128]{2,1,0:T(1,128)S(1)} %tile.9.tile_ref, bf16[128,256]{1,0:T(8,128)(2,1)S(1)} %copy-done.4), custom_call_target="tpu_custom_call" | custom-call | tf_op jit(solution)/shard_map/routing/pallas_call | solution.py:275
  38.0 0.6 slice_bitcast_fusion.2
  38.6 16.3 %owner_gather.2 = (f32[9,128,128]{2,1,0:T(8,128)S(1)}, f32[2,128,128]{2,1,0:T(8,128)S(1)}) custom-call(f32[9,16,128]{2,1,0:T(8,128)S(1)} %constant_dynamic-update-slice_fusion.table_ref, s32[4,128,128]{2,1,0:T(8,128)S(1)} %get-tuple-element.25.asked_ref), custom_call_target="tpu_custom_call" | custom-call | tf_op jit(solution)/shard_map/owner_gather/pallas_call | solution.py:384
  54.9 0.8 copy-done.3
  55.7 35.0 %render.2 = (f32[3,16,256]{2,1,0:T(8,128)}, f32[10,128,128]{2,1,0:T(8,128)}) custom-call(s32[8192]{0:T(1024)} %get-tuple-element.127.slot_ref, f32[9,128,128]{2,1,0:T(8,128)} %copy-done.3, f32[3,16,256]{2,1,0:T(8,128)} %get-tuple-element.115.target_ref, bf16[32,512]{1,0:T(8,128)(2,1)} %constant.106.clone.lines_ref, ...), custom_call_target="tpu_custom_call" | custom-call | tf_op jit(solution)/shard_map/render/pallas_call | solution.py:702
  90.7 1.1 copy-done.1
  91.8 20.4 %owner_scatter.2 = (f32[144,128]{1,0:T(8,128)S(1)}, f32[1,128]{1,0:T(1,128)S(1)}) custom-call(f32[10,128,128]{2,1,0:T(8,128)S(1)} %copy-done.1, f32[2,128,128]{2,1,0:T(8,128)S(1)} %get-tuple-element.28.shift_ref, s32[4,128,128]{2,1,0:T(8,128)S(1)} %get-tuple-element.25.asked_ref), custom_call_target="tpu_custom_call" | custom-call | tf_op jit(solution)/shard_map/owner_scatter/pallas_call | solution.py:503
  112.3 0.1 broadcast_multiply_fusion.1
  112.4 0.0 copy-start.6
  112.4 0.6 slice_divide_fusion.3
  113.0 0.3 slice_divide_fusion.2
  113.3 0.4 fusion.2
  113.7 1.4 fusion.12
  115.2 0.5 divide_subtract_fusion.1
  115.6 0.3 select_multiply_fusion
  116.0 1.6 multiply_select_fusion
  117.6 0.1 multiply_multiply_fusion.9
  117.8 0.2 stack.13
  118.0 0.1 multiply_reduce_fusion.1
  118.1 17.3 %owner_gather.3 = (f32[9,128,128]{2,1,0:T(8,128)S(1)}, f32[2,128,128]{2,1,0:T(8,128)S(1)}) custom-call(f32[9,16,128]{2,1,0:T(8,128)S(1)} %constant_dynamic-update-slice_fusion.7.table_ref, s32[4,128,128]{2,1,0:T(8,128)S(1)} %get-tuple-element.25.asked_ref), custom_call_target="tpu_custom_call" | custom-call | tf_op jit(solution)/shard_map/owner_gather/pallas_call | solution.py:384
  135.4 0.8 copy-done.2
  136.3 35.2 %render.3 = (f32[3,16,256]{2,1,0:T(8,128)}, f32[10,128,128]{2,1,0:T(8,128)}) custom-call(s32[8192]{0:T(1024)} %get-tuple-element.126.slot_ref, f32[9,128,128]{2,1,0:T(8,128)} %copy-done.2, f32[3,16,256]{2,1,0:T(8,128)} %get-tuple-element.114.target_ref, bf16[32,512]{1,0:T(8,128)(2,1)} %constant.106.clone.lines_ref, ...), custom_call_target="tpu_custom_call" | custom-call | tf_op jit(solution)/shard_map/render/pallas_call | solution.py:702
  171.4 1.1 copy-done
  172.5 20.6 %owner_scatter.3 = (f32[144,128]{1,0:T(8,128)S(1)}, f32[1,128]{1,0:T(1,128)S(1)}) custom-call(f32[10,128,128]{2,1,0:T(8,128)S(1)} %copy-done, f32[2,128,128]{2,1,0:T(8,128)S(1)} %get-tuple-element.34.shift_ref, s32[4,128,128]{2,1,0:T(8,128)S(1)} %get-tuple-element.25.asked_ref), custom_call_target="tpu_custom_call" | custom-call | tf_op jit(solution)/shard_map/owner_scatter/pallas_call | solution.py:503
  193.2 0.6 maximum_multiply_fusion
  193.9 0.7 pad_maximum_fusion
  194.5 0.1 broadcast_multiply_fusion
  194.6 0.6 slice_divide_fusion.1
  195.2 0.3 slice_divide_fusion
  195.5 0.4 fusion.13
  195.9 1.3 fusion.23
  197.2 1.6 divide_subtract_fusion
  (45 shorter events, 0.3 us)
Async XLA Ops:
  0.6 0.7 copy-start.12
  2.0 0.7 copy-start.13
  4.1 2.9 %copy-start.8 = (f32[2,16,3,256]{3,1,2,0:T(8,128)S(1)}, f32[2,16,3,256]{3,1,2,0:T(8,128)}, u32[]{:S(2)}) copy-start(f32[2,16,3,256]{3,1,2,0:T(8,128)} %param.20) | copy-start | bytes 294916
  4.1 3.9 %copy-start.5 = (f32[55,2048]{1,0:T(8,128)S(1)}, f32[55,2048]{1,0:T(8,128)}, u32[]{:S(2)}) copy-start(f32[55,2048]{1,0:T(8,128)} %param.15) | copy-start | bytes 1351684
  8.1 0.8 copy-start.9
  9.1 0.8 copy-start.4
  54.9 0.8 copy-start.3
  90.7 1.1 copy-start.1
  112.3 2.8 %copy-start.7 = (f32[55,2048]{1,0:T(8,128)S(1)}, f32[55,2048]{1,0:T(8,128)}, u32[]{:S(2)}) copy-start(f32[55,2048]{1,0:T(8,128)} %param.17) | copy-start | bytes 1351684
  112.4 2.7 %copy-start.6 = (f32[55,2048]{1,0:T(8,128)S(1)}, f32[55,2048]{1,0:T(8,128)}, u32[]{:S(2)}) copy-start(f32[55,2048]{1,0:T(8,128)} %param.16) | copy-start | bytes 1351684
  135.4 0.8 copy-start.2
  171.4 1.1 copy-start
  172.5 21.3 %copy-start.10 = (f32[3,16,256]{2,1,0:T(8,128)S(1)}, f32[3,16,256]{2,1,0:T(8,128)}, u32[]{:S(2)}) copy-start(f32[3,16,256]{2,1,0:T(8,128)} %get-tuple-element.37) | copy-start | bytes 147460
  172.5 21.3 %copy-start.11 = (f32[3,16,256]{2,1,0:T(8,128)S(1)}, f32[3,16,256]{2,1,0:T(8,128)}, u32[]{:S(2)}) copy-start(f32[3,16,256]{2,1,0:T(8,128)} %get-tuple-element.38) | copy-start | bytes 147460

commit v4 on v3

--- a/solution.py
+++ b/solution.py
@@ -138,20 +138,21 @@
     return (device // inner, lax.rem(device, inner))
 
 
-def greet():
-    barrier = pltpu.get_barrier_semaphore()
-    me = my_index()
-
+def greet_one(k):
+    pl.semaphore_signal(
+        pltpu.get_barrier_semaphore(),
+        inc=1,
+        device_id=mesh_place(lax.rem(my_index() + k, OWN)),
+        device_id_type=pl.DeviceIdType.MESH,
+    )
+
+
+def greet(first=1):
     def one(k, _):
-        pl.semaphore_signal(
-            barrier,
-            inc=1,
-            device_id=mesh_place(lax.rem(me + k, OWN)),
-            device_id_type=pl.DeviceIdType.MESH,
-        )
+        greet_one(k)
         return 0
 
-    lax.fori_loop(1, OWN, one, 0, unroll=2)
+    lax.fori_loop(first, OWN, one, 0)
 
 
 def all_entered():
@@ -198,7 +199,9 @@
 
 
 def routing_kernel(ids_ref, tile_ref, upper_ref, slot_ref, asked_ref, request, send_sem, recv_sem):
-    greet()
+    turns = SLABS // GROUP
+    told = (OWN - 1) // turns
+    greet(turns * told + 1)
     row_iota = lax.broadcasted_iota(I32, (OWN, LANES), 0)
     own_tile = (lax.broadcasted_iota(I32, (1, LANES), 1) & (TILES_DEV - 1)).astype(F32)
     zero = jnp.zeros((OWN, LANES), F32)
@@ -206,6 +209,8 @@
 
     def body(k, carry):
         out = []
+        for j in range(told):
+            greet_one(k * told + 1 + j)
         for s in range(STEPS):
             counts, acc = carry[s]
             members, cells = [], []
@@ -243,7 +248,7 @@
         return tuple(out)
 
     start = tuple((zero, jnp.zeros((OWN, 2 * LANES), F32)) for _ in range(STEPS))
-    done = lax.fori_loop(0, SLABS // GROUP, body, start)
+    done = lax.fori_loop(0, turns, body, start)
     for s in range(STEPS):
         acc = done[s][1].astype(I32)
         high = acc[:, LANES:]
@@ -296,14 +301,16 @@
 def gather_kernel(
     step, table_ref, asked_ref, out_ref, shift_ref, parts, got, answer, send_sem, recv_sem
 ):
-    greet()
+    groups = OWN // BLOCKS
+    half = groups // 2
+    told = (OWN - 1) // half
+    greet(half * told + 1)
     for f in range(FIELDS):
         for p, part in enumerate(split3(table_ref[f])):
             parts[f * 16 : f * 16 + 16, p * 128 : p * 128 + 128] = part.astype(BF16)
     low_iota = lax.broadcasted_iota(I32, (128, 256), 0)
     high_iota = lax.broadcasted_iota(I32, (16, 256), 0)
     me = my_index()
-    groups = OWN // BLOCKS
 
     def group_of(k):
         return lax.rem(me // BLOCKS + k, groups)
@@ -348,10 +355,11 @@
             send(answer, out_ref, peer, send_sem, recv_sem)
 
     def early(k, _):
+        for j in range(told):
+            greet_one(k * told + 1 + j)
         compute(group_of(k))
         return 0
 
-    half = groups // 2
     lax.fori_loop(0, half, early, 0)
     all_entered()
 

time: 199 us -> 207 us (1.040)
  Pallas kernels: 173 us -> 181 us
    pallas_call x2, Pallas kernels: 33.6 us -> 39.2 us  [owner_gather(): pl.pallas_call(functools.partial(gather_kernel, step), out_shape=(jax.Sha...]
where the time goes in v4:
time: 207 us
  Pallas kernels  181 us (87%)
  other arithmetic  15.3 us (7%)
  local copies, waits for them, and re-layouts  9.65 us (5%)
    pallas_call x2, Pallas kernels, render(): pl.pallas_call(render_kernel, out_shape=(jax.ShapeDtypeStruct((3, TILES_D...  70.1 us
    pallas_call x2, Pallas kernels, owner_scatter(): pl.pallas_call(functools.partial(scatter_kernel, step), out_shape=(jax.Sh...  42.3 us
    pallas_call x2, Pallas kernels, owner_gather(): pl.pallas_call(functools.partial(gather_kernel, step), out_shape=(jax.Sha...  39.2 us
    pallas_call x1, Pallas kernels, routing(): pl.pallas_call(routing_kernel, out_shape=(jax.ShapeDtypeStruct((STEPS, SL...  29.2 us
    unnamed x38, local copies, waits for them, and re-layouts  6.7 us
    select_n x2, other arithmetic, factor_rows(): beta = jnp.where(has_a, half_log2e * conic_b / root, 0.0)  4.36 us

profile of v4, /device:TPU:1, one launch (start us, length us, event | category | flops | bytes accessed | tf_op | source)
XLA Modules:
  0.0 206.9 jit_solution(12450323705081259129)
XLA Ops:
  0.6 0.7 copy-done.12
  1.3 0.7 fusion.81
  2.0 0.7 copy-done.13
  2.7 0.1 tile.9.tile_ref
  2.7 1.3 select_multiply_fusion.1
  4.1 0.0 copy-start.8
  4.1 2.8 %multiply_select_fusion.2 = (f32[1,2048]{1,0:T(1,128)S(1)}, f32[1,2048]{1,0:T(1,128)S(1)}, f32[1,2048]{1,0:T(1,128)S(1)}, f32[1,2048]{1,0:T(1,128)S(1)}, f32[1,2...) fusion(f32[1,2048]{1,0:T(1,128)S(1)} %get-tuple-element.83, ...), kind=kLoop, calls=%fused_computation.162 | loop fusion | flops 63488 | bytes 147464 | tf_op jit(solution)/shard_map/jit(_where)/select_n | solution.py:115
  7.0 0.6 slice_bitcast_fusion
  7.6 0.1 multiply_multiply_fusion.18
  7.7 0.2 stack.12
  8.0 0.1 multiply_reduce_fusion.3
  8.1 0.8 copy-done.9
  8.9 0.2 copy.20
  9.1 0.0 copy-start.4
  9.1 0.2 reshape.208.ids_ref
  9.3 0.6 copy-done.4
  10.0 29.2 %routing.1 = (s32[2,64,128]{2,1,0:T(8,128)S(1)}, s32[4,128,128]{2,1,0:T(8,128)S(1)}) custom-call(s32[2,64,128]{2,1,0:T(8,128)S(1)} %reshape.208.ids_ref, s32[2,1,128]{2,1,0:T(1,128)S(1)} %tile.9.tile_ref, bf16[128,256]{1,0:T(8,128)(2,1)S(1)} %copy-done.4), custom_call_target="tpu_custom_call" | custom-call | tf_op jit(solution)/shard_map/routing/pallas_call | solution.py:280
  39.2 0.6 slice_bitcast_fusion.2
  39.8 19.0 %owner_gather.2 = (f32[9,128,128]{2,1,0:T(8,128)S(1)}, f32[2,128,128]{2,1,0:T(8,128)S(1)}) custom-call(f32[9,16,128]{2,1,0:T(8,128)S(1)} %constant_dynamic-update-slice_fusion.table_ref, s32[4,128,128]{2,1,0:T(8,128)S(1)} %get-tuple-element.25.asked_ref), custom_call_target="tpu_custom_call" | custom-call | tf_op jit(solution)/shard_map/owner_gather/pallas_call | solution.py:392
  58.8 0.8 copy-done.3
  59.6 35.0 %render.2 = (f32[3,16,256]{2,1,0:T(8,128)}, f32[10,128,128]{2,1,0:T(8,128)}) custom-call(s32[8192]{0:T(1024)} %get-tuple-element.127.slot_ref, f32[9,128,128]{2,1,0:T(8,128)} %copy-done.3, f32[3,16,256]{2,1,0:T(8,128)} %get-tuple-element.115.target_ref, bf16[32,512]{1,0:T(8,128)(2,1)} %constant.106.clone.lines_ref, ...), custom_call_target="tpu_custom_call" | custom-call | tf_op jit(solution)/shard_map/render/pallas_call | solution.py:710
  94.6 1.1 copy-done.1
  95.7 20.5 %owner_scatter.2 = (f32[144,128]{1,0:T(8,128)S(1)}, f32[1,128]{1,0:T(1,128)S(1)}) custom-call(f32[10,128,128]{2,1,0:T(8,128)S(1)} %copy-done.1, f32[2,128,128]{2,1,0:T(8,128)S(1)} %get-tuple-element.28.shift_ref, s32[4,128,128]{2,1,0:T(8,128)S(1)} %get-tuple-element.25.asked_ref), custom_call_target="tpu_custom_call" | custom-call | tf_op jit(solution)/shard_map/owner_scatter/pallas_call | solution.py:511
  116.3 0.1 broadcast_multiply_fusion.1
  116.4 0.0 copy-start.6
  116.4 0.6 slice_divide_fusion.3
  117.0 0.3 slice_divide_fusion.2
  117.3 0.4 fusion.2
  117.7 1.4 fusion.12
  119.1 0.5 divide_subtract_fusion.1
  119.6 0.3 select_multiply_fusion
  119.9 1.6 multiply_select_fusion
  121.6 0.1 multiply_multiply_fusion.9
  121.7 0.2 stack.13
  122.0 0.1 multiply_reduce_fusion.1
  122.1 20.2 %owner_gather.3 = (f32[9,128,128]{2,1,0:T(8,128)S(1)}, f32[2,128,128]{2,1,0:T(8,128)S(1)}) custom-call(f32[9,16,128]{2,1,0:T(8,128)S(1)} %constant_dynamic-update-slice_fusion.7.table_ref, s32[4,128,128]{2,1,0:T(8,128)S(1)} %get-tuple-element.25.asked_ref), custom_call_target="tpu_custom_call" | custom-call | tf_op jit(solution)/shard_map/owner_gather/pallas_call | solution.py:392
  142.3 0.8 copy-done.2
  143.2 35.2 %render.3 = (f32[3,16,256]{2,1,0:T(8,128)}, f32[10,128,128]{2,1,0:T(8,128)}) custom-call(s32[8192]{0:T(1024)} %get-tuple-element.126.slot_ref, f32[9,128,128]{2,1,0:T(8,128)} %copy-done.2, f32[3,16,256]{2,1,0:T(8,128)} %get-tuple-element.114.target_ref, bf16[32,512]{1,0:T(8,128)(2,1)} %constant.106.clone.lines_ref, ...), custom_call_target="tpu_custom_call" | custom-call | tf_op jit(solution)/shard_map/render/pallas_call | solution.py:710
  178.3 1.1 copy-done
  179.4 21.8 %owner_scatter.3 = (f32[144,128]{1,0:T(8,128)S(1)}, f32[1,128]{1,0:T(1,128)S(1)}) custom-call(f32[10,128,128]{2,1,0:T(8,128)S(1)} %copy-done, f32[2,128,128]{2,1,0:T(8,128)S(1)} %get-tuple-element.34.shift_ref, s32[4,128,128]{2,1,0:T(8,128)S(1)} %get-tuple-element.25.asked_ref), custom_call_target="tpu_custom_call" | custom-call | tf_op jit(solution)/shard_map/owner_scatter/pallas_call | solution.py:511
  201.2 0.6 maximum_multiply_fusion
  201.9 0.7 pad_maximum_fusion
  202.5 0.1 broadcast_multiply_fusion
  202.6 0.6 slice_divide_fusion.1
  203.2 0.3 slice_divide_fusion
  203.5 0.4 fusion.13
  203.9 1.3 fusion.23
  205.2 1.6 divide_subtract_fusion
  (45 shorter events, 0.3 us)
Async XLA Ops:
  0.6 0.7 copy-start.12
  2.0 0.7 copy-start.13
  4.1 2.9 %copy-start.8 = (f32[2,16,3,256]{3,1,2,0:T(8,128)S(1)}, f32[2,16,3,256]{3,1,2,0:T(8,128)}, u32[]{:S(2)}) copy-start(f32[2,16,3,256]{3,1,2,0:T(8,128)} %param.20) | copy-start | bytes 294916
  4.1 3.9 %copy-start.5 = (f32[55,2048]{1,0:T(8,128)S(1)}, f32[55,2048]{1,0:T(8,128)}, u32[]{:S(2)}) copy-start(f32[55,2048]{1,0:T(8,128)} %param.15) | copy-start | bytes 1351684
  8.1 0.8 copy-start.9
  9.1 0.8 copy-start.4
  58.8 0.8 copy-start.3
  94.6 1.1 copy-start.1
  116.3 2.8 %copy-start.7 = (f32[55,2048]{1,0:T(8,128)S(1)}, f32[55,2048]{1,0:T(8,128)}, u32[]{:S(2)}) copy-start(f32[55,2048]{1,0:T(8,128)} %param.17) | copy-start | bytes 1351684
  116.4 2.7 %copy-start.6 = (f32[55,2048]{1,0:T(8,128)S(1)}, f32[55,2048]{1,0:T(8,128)}, u32[]{:S(2)}) copy-start(f32[55,2048]{1,0:T(8,128)} %param.16) | copy-start | bytes 1351684
  142.3 0.8 copy-start.2
  178.3 1.1 copy-start
  179.4 22.4 %copy-start.10 = (f32[3,16,256]{2,1,0:T(8,128)S(1)}, f32[3,16,256]{2,1,0:T(8,128)}, u32[]{:S(2)}) copy-start(f32[3,16,256]{2,1,0:T(8,128)} %get-tuple-element.37) | copy-start | bytes 147460
  179.4 22.4 %copy-start.11 = (f32[3,16,256]{2,1,0:T(8,128)S(1)}, f32[3,16,256]{2,1,0:T(8,128)}, u32[]{:S(2)}) copy-start(f32[3,16,256]{2,1,0:T(8,128)} %get-tuple-element.38) | copy-start | bytes 147460

commit v5 on v3

--- a/solution.py
+++ b/solution.py
@@ -138,43 +138,68 @@
     return (device // inner, lax.rem(device, inner))
 
 
+CHIPS = OWN // 2
+
+
+def my_chip_core():
+    me = my_index()
+    return me // 2, lax.rem(me, 2)
+
+
 def greet():
     barrier = pltpu.get_barrier_semaphore()
-    me = my_index()
-
-    def one(k, _):
+    chip, core = my_chip_core()
+
+    def tell(device):
         pl.semaphore_signal(
             barrier,
             inc=1,
-            device_id=mesh_place(lax.rem(me + k, OWN)),
+            device_id=mesh_place(device),
             device_id_type=pl.DeviceIdType.MESH,
         )
+
+    tell(2 * chip + 1 - core)
+
+    def one(k, _):
+        tell(2 * lax.rem(chip + k, CHIPS) + core)
         return 0
 
-    lax.fori_loop(1, OWN, one, 0, unroll=2)
+    lax.fori_loop(1, CHIPS, one, 0, unroll=3)
 
 
 def all_entered():
-    pl.semaphore_wait(pltpu.get_barrier_semaphore(), OWN - 1)
-
-
-def send(source, target, peer, send_sem, recv_sem):
-    me = my_index()
-    pltpu.make_async_remote_copy(
-        src_ref=source.at[:, peer, :],
-        dst_ref=target.at[:, me, :],
+    pl.semaphore_wait(pltpu.get_barrier_semaphore(), CHIPS)
+
+
+def to_sibling(source, mixed, send_sem, recv_sem):
+    chip, core = my_chip_core()
+    return pltpu.make_async_remote_copy(
+        src_ref=source,
+        dst_ref=mixed.at[:, core, :, :],
         send_sem=send_sem,
         recv_sem=recv_sem,
-        device_id=mesh_place(peer),
+        device_id=mesh_place(2 * chip + 1 - core),
+        device_id_type=pl.DeviceIdType.MESH,
+    )
+
+
+def to_chip(peer, mixed, target, send_sem, recv_sem):
+    chip, core = my_chip_core()
+    pltpu.make_async_remote_copy(
+        src_ref=mixed.at[:, :, peer, :],
+        dst_ref=target.at[:, :, chip, :],
+        send_sem=send_sem,
+        recv_sem=recv_sem,
+        device_id=mesh_place(2 * peer + core),
         device_id_type=pl.DeviceIdType.MESH,
     ).start()
 
 
-def all_but_one(source, target, send_sem, recv_sem):
-    blocks = pl.ds(0, OWN - 1)
+def bytes_of(first, count, mixed, target, send_sem, recv_sem):
+    chips = pl.ds(first, count)
     return pltpu.make_async_remote_copy(
-        src_ref=source.at[:, blocks, :],
-        dst_ref=target.at[:, blocks, :],
+        src_ref=mixed.at[:, :, chips, :],
+        dst_ref=target.at[:, :, chips, :],
         send_sem=send_sem,
         recv_sem=recv_sem,
         device_id=mesh_place(my_index()),
@@ -182,10 +207,11 @@
     )
 
 
-def keep_own(source, target):
-    me = my_index()
-    for k in range(source.shape[0]):
-        target[k, pl.ds(me, 1), :] = source[k, pl.ds(me, 1), :]
+def keep_own(mixed, target):
+    chip, _ = my_chip_core()
+    for k in range(mixed.shape[0]):
+        for core in range(2):
+            target[k, core, pl.ds(chip, 1), :] = mixed[k, core, pl.ds(chip, 1), :]
 
 
 def remote_params(collective_id, megabytes=32):
@@ -197,7 +223,9 @@
 GROUP = 4
 
 
-def routing_kernel(ids_ref, tile_ref, upper_ref, slot_ref, asked_ref, request, send_sem, recv_sem):
+def routing_kernel(ids_ref, tile_ref, upper_ref, slot_ref, asked_ref, request, mixed, send_sem, recv_sem,
+    near_send, near_recv,
+):
     greet()
     row_iota = lax.broadcasted_iota(I32, (OWN, LANES), 0)
     own_tile = (lax.broadcasted_iota(I32, (1, LANES), 1) & (TILES_DEV - 1)).astype(F32)
@@ -211,7 +239,7 @@
             members, cells = [], []
             for c in range(GROUP):
                 ids = ids_ref[s, pl.ds(k * GROUP + c, 1), :]
-                owner = lax.shift_right_logical(ids, 11)
+                owner = lax.shift_right_logical(ids, 12) + (lax.shift_right_logical(ids, 11) & 1) * CHIPS
                 member = row_iota == owner
                 member_bf = jnp.where(member, 1.0, 0.0).astype(BF16)
                 ahead = jnp.dot(member_bf, upper, preferred_element_type=F32)
@@ -247,23 +275,30 @@
     for s in range(STEPS):
         acc = done[s][1].astype(I32)
         high = acc[:, LANES:]
-        request[s] = acc[:, :LANES] + lax.shift_right_logical(high, 4) * 128
-        request[STEPS + s] = jnp.take_along_axis(
+        want = acc[:, :LANES] + lax.shift_right_logical(high, 4) * 128
+        request[s] = want.reshape(2, CHIPS, LANES)
+        tile = jnp.take_along_axis(
             jnp.broadcast_to(tile_ref[s], (OWN, LANES)),
             high & 15,
             axis=1,
             mode="promise_in_bounds",
         )
+        request[STEPS + s] = tile.reshape(2, CHIPS, LANES)
     all_entered()
-    me = my_index()
+    chip, core = my_chip_core()
+    near = to_sibling(request.at[:, 1 - core, :, :], mixed, near_send, near_recv)
+    near.start()
+    for k in range(2 * STEPS):
+        mixed[k, core] = request[k, core]
+    near.wait()
 
     def push(k, _):
-        send(request, asked_ref, lax.rem(me + k, OWN), send_sem, recv_sem)
+        to_chip(lax.rem(chip + k, CHIPS), mixed, asked_ref, send_sem, recv_sem)
         return 0
 
-    lax.fori_loop(1, OWN, push, 0, unroll=2)
-    keep_own(request, asked_ref)
-    rest = all_but_one(request, asked_ref, send_sem, recv_sem)
+    lax.fori_loop(1, CHIPS, push, 0, unroll=3)
+    keep_own(mixed, asked_ref)
+    rest = bytes_of(0, CHIPS - 1, mixed, asked_ref, send_sem, recv_sem)
     rest.wait_send()
     rest.wait_recv()
 
@@ -276,12 +311,15 @@
         routing_kernel,
         out_shape=(
             jax.ShapeDtypeStruct((STEPS, SLABS, LANES), I32),
-            jax.ShapeDtypeStruct((2 * STEPS, OWN, LANES), I32),
+            jax.ShapeDtypeStruct((2 * STEPS, 2, CHIPS, LANES), I32),
         ),
         in_specs=[vmem] * 3,
         out_specs=(vmem, vmem),
         scratch_shapes=[
-            pltpu.VMEM((2 * STEPS, OWN, LANES), I32),
+            pltpu.VMEM((2 * STEPS, 2, CHIPS, LANES), I32),
+            pltpu.VMEM((2 * STEPS, 2, CHIPS, LANES), I32),
+            pltpu.SemaphoreType.DMA,
+            pltpu.SemaphoreType.DMA,
             pltpu.SemaphoreType.DMA,
             pltpu.SemaphoreType.DMA,
         ],
@@ -294,7 +332,8 @@
 
 
 def gather_kernel(
-    step, table_ref, asked_ref, out_ref, shift_ref, parts, got, answer, send_sem, recv_sem
+    step, table_ref, asked_ref, out_ref, shift_ref, parts, got, answer, mixed, send_sem, recv_sem,
+    near_send, near_recv,
 ):
     greet()
     for f in range(FIELDS):
@@ -302,14 +341,14 @@
             parts[f * 16 : f * 16 + 16, p * 128 : p * 128 + 128] = part.astype(BF16)
     low_iota = lax.broadcasted_iota(I32, (128, 256), 0)
     high_iota = lax.broadcasted_iota(I32, (16, 256), 0)
-    me = my_index()
-    groups = OWN // BLOCKS
+    chip, core = my_chip_core()
+    groups = CHIPS // BLOCKS
 
     def group_of(k):
-        return lax.rem(me // BLOCKS + k, groups)
-
-    def compute(group):
-        first = pl.multiple_of(group * BLOCKS, BLOCKS)
+        return lax.rem(chip // BLOCKS + k, groups)
+
+    def compute(group, receiver):
+        first = pl.multiple_of(receiver * CHIPS + group * BLOCKS, BLOCKS)
         for pair in range(BLOCKS // 2):
             d = first + 2 * pair
             want = jnp.concatenate(
@@ -334,47 +373,66 @@
         shift_ref[0, at, :] = local_u
         shift_ref[1, at, :] = local_v
         alpha, beta, gamma = got[2], got[3], got[4]
-        answer[0, at, :] = alpha
-        answer[1, at, :] = beta
-        answer[2, at, :] = gamma
-        answer[3, at, :] = -(alpha * local_u + beta * local_v)
-        answer[4, at, :] = -gamma * local_v
-        for f in range(5, FIELDS):
-            answer[f, at, :] = got[f]
+        chips = pl.ds(pl.multiple_of(group * BLOCKS, BLOCKS), BLOCKS)
+        values = [
+            alpha,
+            beta,
+            gamma,
+            -(alpha * local_u + beta * local_v),
+            -gamma * local_v,
+            *[got[f] for f in range(5, FIELDS)],
+        ]
+        return chips, values
+
+    def others(k, _):
+        chips, values = compute(group_of(k), 1 - core)
+        for f in range(FIELDS):
+            answer[f, chips, :] = values[f]
+        return 0
+
+    lax.fori_loop(0, groups, others, 0)
+    all_entered()
+    near = to_sibling(answer, mixed, near_send, near_recv)
+    near.start()
+
+    def ours(k):
+        chips, values = compute(group_of(k), core)
+        for f in range(FIELDS):
+            mixed[f, core, chips, :] = values[f]
 
     def push(group):
         for k in range(BLOCKS):
-            peer = group * BLOCKS + lax.rem(me + k, BLOCKS)
-            send(answer, out_ref, peer, send_sem, recv_sem)
+            peer = group * BLOCKS + lax.rem(chip + k, BLOCKS)
+            to_chip(peer, mixed, out_ref, send_sem, recv_sem)
 
     def early(k, _):
-        compute(group_of(k))
+        ours(k)
         return 0
 
-    half = groups // 2
-    lax.fori_loop(0, half, early, 0)
-    all_entered()
+    lax.fori_loop(0, groups // 2, early, 0)
+    near.wait()
 
     def late(k, _):
-        push(group_of(2 * k + 1))
-        push(group_of(2 * k + 2))
-        compute(group_of(k + half))
+        push(group_of(k - groups // 2 + 1))
+        ours(k)
         return 0
 
-    lax.fori_loop(0, half - 2, late, 0)
-    compute(group_of(groups - 2))
-    push(group_of(groups - 3))
-    compute(group_of(groups - 1))
-    push(group_of(groups - 2))
-    push(group_of(groups - 1))
+    lax.fori_loop(groups // 2, groups, late, 0)
+
+    def last(k, _):
+        push(group_of(k))
+        return 0
+
+    lax.fori_loop(groups // 2 + 1, groups, last, 0)
 
     def inside(k, _):
-        send(answer, out_ref, me // BLOCKS * BLOCKS + lax.rem(me + k, BLOCKS), send_sem, recv_sem)
+        peer = chip // BLOCKS * BLOCKS + lax.rem(chip + k, BLOCKS)
+        to_chip(peer, mixed, out_ref, send_sem, recv_sem)
         return 0
 
     lax.fori_loop(1, BLOCKS, inside, 0)
-    keep_own(answer, out_ref)
-    rest = all_but_one(answer, out_ref, send_sem, recv_sem)
+    keep_own(mixed, out_ref)
+    rest = bytes_of(0, CHIPS - 1, mixed, out_ref, send_sem, recv_sem)
     rest.wait_send()
     rest.wait_recv()
 
@@ -384,7 +442,7 @@
     return pl.pallas_call(
         functools.partial(gather_kernel, step),
         out_shape=(
-            jax.ShapeDtypeStruct((FIELDS, OWN, LANES), F32),
+            jax.ShapeDtypeStruct((FIELDS, 2, CHIPS, LANES), F32),
             jax.ShapeDtypeStruct((2, OWN, LANES), F32),
         ),
         in_specs=[vmem] * 2,
@@ -392,7 +450,10 @@
         scratch_shapes=[
             pltpu.VMEM((FIELDS * 16, 384), BF16),
             pltpu.VMEM((FIELDS, BLOCKS, LANES), F32),
-            pltpu.VMEM((FIELDS, OWN, LANES), F32),
+            pltpu.VMEM((FIELDS, CHIPS, LANES), F32),
+            pltpu.VMEM((FIELDS, 2, CHIPS, LANES), F32),
+            pltpu.SemaphoreType.DMA,
+            pltpu.SemaphoreType.DMA,
             pltpu.SemaphoreType.DMA,
             pltpu.SemaphoreType.DMA,
         ],
@@ -403,35 +464,31 @@
 
 def scatter_kernel(
     step, moment_ref, shift_ref, asked_ref, out_ref, loss_ref,
-    arrived, high, rest, own_sem, send_sem, recv_sems,
+    arrived, high, rest, mixed, near_send, near_recv, send_sem, recv_sems,
 ):
     greet()
-    me = my_index()
-    groups = OWN // BLOCKS
-    mine = me // BLOCKS
+    chip, core = my_chip_core()
+    groups = CHIPS // BLOCKS
+    mine = chip // BLOCKS
     all_entered()
+    near = to_sibling(moment_ref.at[:, 1 - core, :, :], mixed, near_send, near_recv)
+    near.start()
+    for k in range(FIELDS + 1):
+        mixed[k, core] = moment_ref[k, core]
+    near.wait()
 
     def push(k, _):
-        send(moment_ref, arrived, lax.rem(me + k, OWN), send_sem, recv_sems.at[mine])
+        to_chip(lax.rem(chip + k, CHIPS), mixed, arrived, send_sem, recv_sems.at[mine])
         return 0
 
-    lax.fori_loop(1, OWN, push, 0, unroll=2)
-    own = pltpu.make_async_copy(moment_ref.at[:, me, :], arrived.at[:, me, :], own_sem)
-    own.start()
-    own.wait()
+    lax.fori_loop(1, CHIPS, push, 0, unroll=3)
+    keep_own(mixed, arrived)
     low_iota = lax.broadcasted_iota(I32, (128, 128), 0)
     high_iota = lax.broadcasted_iota(I32, (16, 128), 0)
 
     def landed(group, count):
-        blocks = pl.ds(group * BLOCKS, count)
-        pltpu.make_async_remote_copy(
-            src_ref=moment_ref.at[:, blocks, :],
-            dst_ref=arrived.at[:, blocks, :],
-            send_sem=send_sem,
-            recv_sem=recv_sems.at[group],
-            device_id=mesh_place(me),
-            device_id_type=pl.DeviceIdType.MESH,
-        ).wait_recv()
+        first = group * BLOCKS
+        bytes_of(first, count, mixed, arrived, send_sem, recv_sems.at[group]).wait_recv()
 
     def body(k, carry):
         acc, loss = carry
@@ -445,47 +502,50 @@
         def _():
             landed(group, BLOCKS)
 
-        first = pl.multiple_of(group * BLOCKS, BLOCKS)
-        at = pl.ds(first, BLOCKS)
-        local_u, local_v = shift_ref[0, at, :], shift_ref[1, at, :]
-        m0, mx, my = arrived[0, at, :], arrived[1, at, :], arrived[2, at, :]
-        sx = mx - local_u * m0
-        sy = my - local_v * m0
-        sums = [
-            sx,
-            sy,
-            arrived[3, at, :] - local_u * (mx + sx),
-            arrived[4, at, :] - local_u * my - local_v * sx,
-            arrived[5, at, :] - local_v * (my + sy),
-            m0,
-            arrived[6, at, :],
-            arrived[7, at, :],
-            arrived[8, at, :],
-        ]
-        for f in range(FIELDS):
-            top = sums[f].astype(BF16).astype(F32)
-            high[f] = top
-            rest[f] = sums[f] - top
-        for pair in range(BLOCKS // 2):
-            lefts, rights = [], []
-            for half in range(2):
-                d = 2 * pair + half
-                want = asked_ref[step, pl.ds(first + d, 1), :]
-                rights.append(jnp.where(low_iota == (want & 127), 1.0, 0.0).astype(BF16))
-                here = high_iota == lax.shift_right_logical(want, 7)
-                rows = [
-                    jnp.where(here, ref[f, d : d + 1, :], 0.0).astype(BF16)
-                    for ref in (high, rest)
-                    for f in range(FIELDS)
-                ]
-                lefts.append(jnp.concatenate(rows, 0))
-            acc = acc + lax.dot_general(
-                jnp.concatenate(lefts, 1),
-                jnp.concatenate(rights, 1),
-                (((1,), (1,)), ((), ())),
-                preferred_element_type=F32,
-            )
-        return acc, loss + arrived[FIELDS, at, :]
+        for sender in range(2):
+            chips = pl.ds(pl.multiple_of(group * BLOCKS, BLOCKS), BLOCKS)
+            first = pl.multiple_of(sender * CHIPS + group * BLOCKS, BLOCKS)
+            at = pl.ds(first, BLOCKS)
+            local_u, local_v = shift_ref[0, at, :], shift_ref[1, at, :]
+            m0, mx, my = arrived[0, sender, chips, :], arrived[1, sender, chips, :], arrived[2, sender, chips, :]
+            sx = mx - local_u * m0
+            sy = my - local_v * m0
+            sums = [
+                sx,
+                sy,
+                arrived[3, sender, chips, :] - local_u * (mx + sx),
+                arrived[4, sender, chips, :] - local_u * my - local_v * sx,
+                arrived[5, sender, chips, :] - local_v * (my + sy),
+                m0,
+                arrived[6, sender, chips, :],
+                arrived[7, sender, chips, :],
+                arrived[8, sender, chips, :],
+            ]
+            for f in range(FIELDS):
+                top = sums[f].astype(BF16).astype(F32)
+                high[f] = top
+                rest[f] = sums[f] - top
+            for pair in range(BLOCKS // 2):
+                lefts, rights = [], []
+                for half in range(2):
+                    d = 2 * pair + half
+                    want = asked_ref[step, pl.ds(first + d, 1), :]
+                    rights.append(jnp.where(low_iota == (want & 127), 1.0, 0.0).astype(BF16))
+                    here = high_iota == lax.shift_right_logical(want, 7)
+                    rows = [
+                        jnp.where(here, ref[f, d : d + 1, :], 0.0).astype(BF16)
+                        for ref in (high, rest)
+                        for f in range(FIELDS)
+                    ]
+                    lefts.append(jnp.concatenate(rows, 0))
+                acc = acc + lax.dot_general(
+                    jnp.concatenate(lefts, 1),
+                    jnp.concatenate(rights, 1),
+                    (((1,), (1,)), ((), ())),
+                    preferred_element_type=F32,
+                )
+            loss = loss + arrived[FIELDS, sender, chips, :]
+        return acc, loss
 
     acc, loss = lax.fori_loop(
         0,
@@ -495,7 +555,7 @@
     )
     out_ref[...] = acc[: FIELDS * 16] + acc[FIELDS * 16 :]
     loss_ref[...] = jnp.sum(loss, axis=0, keepdims=True)
-    all_but_one(moment_ref, arrived, send_sem, own_sem).wait_send()
+    bytes_of(0, CHIPS - 1, mixed, arrived, send_sem, near_recv).wait_send()
 
 
 def owner_scatter(step, moments, shifts, asked):
@@ -509,12 +569,14 @@
         in_specs=[vmem] * 3,
         out_specs=(vmem, vmem),
         scratch_shapes=[
-            pltpu.VMEM((FIELDS + 1, OWN, LANES), F32),
+            pltpu.VMEM((FIELDS + 1, 2, CHIPS, LANES), F32),
             pltpu.VMEM((FIELDS, BLOCKS, LANES), F32),
             pltpu.VMEM((FIELDS, BLOCKS, LANES), F32),
-            pltpu.SemaphoreType.DMA,
-            pltpu.SemaphoreType.DMA,
-            pltpu.SemaphoreType.DMA((OWN // BLOCKS,)),
+            pltpu.VMEM((FIELDS + 1, 2, CHIPS, LANES), F32),
+            pltpu.SemaphoreType.DMA,
+            pltpu.SemaphoreType.DMA,
+            pltpu.SemaphoreType.DMA,
+            pltpu.SemaphoreType.DMA((CHIPS // BLOCKS,)),
         ],
         compiler_params=remote_params(1 + STEPS + step),
         name="owner_scatter",
@@ -738,6 +800,7 @@
     lane_tiles = jnp.tile(tile_ids, (1, LANES // TILES_DEV))
     slots, asked = routing(ids, lane_tiles[:, None, :])
     slots = slots.reshape(STEPS, SLABS * LANES)
+    asked = asked.reshape(2 * STEPS, OWN, LANES)
     pictures = []
     losses = []
     for step_index in range(STEPS):
@@ -746,8 +809,10 @@
         )
         table = factor_rows(projected, inverses).reshape(FIELDS, 16, 128)
         fields, shifts = owner_gather(step_index, table, asked)
+        fields = fields.reshape(FIELDS, OWN, LANES)
         target = jnp.swapaxes(targets[step_index], 0, 1)
         picture, moments = render(slots[step_index], fields, target)
+        moments = moments.reshape(FIELDS + 1, 2, CHIPS, LANES)
         sums, loss = owner_scatter(step_index, moments, shifts, asked)
         sums = sums.reshape(FIELDS, local_count)
         losses.append(loss[0, 0])

time: 199 us -> 200 us (level)
    pallas_call x2, Pallas kernels: 41.1 us -> 43.6 us  [owner_scatter(): pl.pallas_call(functools.partial(scatter_kernel, step), out_shape=(jax.Sh...]
where the time goes in v5:
time: 200 us
  Pallas kernels  174 us (87%)
  other arithmetic  15.3 us (8%)
  local copies, waits for them, and re-layouts  9.65 us (5%)
    pallas_call x2, Pallas kernels, render(): pl.pallas_call(render_kernel, out_shape=(jax.ShapeDtypeStruct((3, TILES_D...  70.1 us
    pallas_call x2, Pallas kernels, owner_scatter(): pl.pallas_call(functools.partial(scatter_kernel, step), out_shape=(jax.Sh...  43.6 us
    pallas_call x2, Pallas kernels, owner_gather(): pl.pallas_call(functools.partial(gather_kernel, step), out_shape=(jax.Sha...  33 us
    pallas_call x1, Pallas kernels, routing(): pl.pallas_call(routing_kernel, out_shape=(jax.ShapeDtypeStruct((STEPS, SL...  27.1 us
    unnamed x38, local copies, waits for them, and re-layouts  6.7 us
    select_n x2, other arithmetic, factor_rows(): beta = jnp.where(has_a, half_log2e * conic_b / root, 0.0)  4.36 us

profile of v5, /device:TPU:1, one launch (start us, length us, event | category | flops | bytes accessed | tf_op | source)
XLA Modules:
  0.0 199.8 jit_solution(7903259839824243481)
XLA Ops:
  0.6 0.7 copy-done.12
  1.3 0.7 fusion.81
  2.0 0.7 copy-done.13
  2.7 0.1 tile.9.tile_ref
  2.7 1.3 select_multiply_fusion.1
  4.1 0.0 copy-start.8
  4.1 2.8 %multiply_select_fusion.2 = (f32[1,2048]{1,0:T(1,128)S(1)}, f32[1,2048]{1,0:T(1,128)S(1)}, f32[1,2048]{1,0:T(1,128)S(1)}, f32[1,2048]{1,0:T(1,128)S(1)}, f32[1,2...) fusion(f32[1,2048]{1,0:T(1,128)S(1)} %get-tuple-element.83, ...), kind=kLoop, calls=%fused_computation.162 | loop fusion | flops 63488 | bytes 147464 | tf_op jit(solution)/shard_map/jit(_where)/select_n | solution.py:115
  7.0 0.6 slice_bitcast_fusion
  7.6 0.1 multiply_multiply_fusion.18
  7.7 0.2 stack.12
  8.0 0.1 multiply_reduce_fusion.3
  8.1 0.8 copy-done.9
  8.9 0.2 copy.20
  9.1 0.0 copy-start.4
  9.1 0.2 reshape.223.ids_ref
  9.3 0.6 copy-done.4
  10.0 27.1 %routing.1 = (s32[2,64,128]{2,1,0:T(8,128)S(1)}, s32[4,2,64,128]{3,2,1,0:T(8,128)S(1)}) custom-call(s32[2,64,128]{2,1,0:T(8,128)S(1)} %reshape.223.ids_ref, s32[2,1,128]{2,1,0:T(1,128)S(1)} %tile.9.tile_ref, bf16[128,256]{1,0:T(8,128)(2,1)S(1)} %copy-done.4), custom_call_target="tpu_custom_call" | custom-call | tf_op jit(solution)/shard_map/routing/pallas_call | solution.py:310
  37.1 0.6 slice_bitcast_fusion.2
  37.7 16.6 %owner_gather.2 = (f32[9,2,64,128]{3,2,1,0:T(8,128)S(1)}, f32[2,128,128]{2,1,0:T(8,128)S(1)}) custom-call(f32[9,16,128]{2,1,0:T(8,128)S(1)} %constant_dynamic-update-slice_fusion.table_ref, s32[4,128,128]{2,1,0:T(8,128)S(1)} %bitcast.106), custom_call_target="tpu_custom_call" | custom-call | tf_op jit(solution)/shard_map/owner_gather/pallas_call | solution.py:442
  54.3 0.8 copy-done.3
  55.1 35.0 %render.2 = (f32[3,16,256]{2,1,0:T(8,128)}, f32[10,128,128]{2,1,0:T(8,128)}) custom-call(s32[8192]{0:T(1024)} %get-tuple-element.127.slot_ref, f32[9,128,128]{2,1,0:T(8,128)} %bitcast.113, f32[3,16,256]{2,1,0:T(8,128)} %get-tuple-element.115.target_ref, bf16[32,512]{1,0:T(8,128)(2,1)} %constant.106.clone.lines_ref, ...), custom_call_target="tpu_custom_call" | custom-call | tf_op jit(solution)/shard_map/render/pallas_call | solution.py:764
  90.1 1.1 copy-done.1
  91.2 21.9 %owner_scatter.2 = (f32[144,128]{1,0:T(8,128)S(1)}, f32[1,128]{1,0:T(1,128)S(1)}) custom-call(f32[10,2,64,128]{3,2,1,0:T(8,128)S(1)} %bitcast.111, f32[2,128,128]{2,1,0:T(8,128)S(1)} %get-tuple-element.28.shift_ref, s32[4,128,128]{2,1,0:T(8,128)S(1)} %bitcast.107), custom_call_target="tpu_custom_call" | custom-call | tf_op jit(solution)/shard_map/owner_scatter/pallas_call | solution.py:563
  113.2 0.1 broadcast_multiply_fusion.1
  113.3 0.0 copy-start.6
  113.3 0.6 slice_divide_fusion.3
  113.9 0.3 slice_divide_fusion.2
  114.2 0.4 fusion.2
  114.6 1.4 fusion.12
  116.0 0.5 divide_subtract_fusion.1
  116.5 0.3 select_multiply_fusion
  116.8 1.6 multiply_select_fusion
  118.5 0.1 multiply_multiply_fusion.9
  118.6 0.2 stack.13
  118.9 0.1 multiply_reduce_fusion.1
  119.0 16.4 %owner_gather.3 = (f32[9,2,64,128]{3,2,1,0:T(8,128)S(1)}, f32[2,128,128]{2,1,0:T(8,128)S(1)}) custom-call(f32[9,16,128]{2,1,0:T(8,128)S(1)} %constant_dynamic-update-slice_fusion.7.table_ref, s32[4,128,128]{2,1,0:T(8,128)S(1)} %bitcast.108), custom_call_target="tpu_custom_call" | custom-call | tf_op jit(solution)/shard_map/owner_gather/pallas_call | solution.py:442
  135.4 0.8 copy-done.2
  136.2 35.1 %render.3 = (f32[3,16,256]{2,1,0:T(8,128)}, f32[10,128,128]{2,1,0:T(8,128)}) custom-call(s32[8192]{0:T(1024)} %get-tuple-element.126.slot_ref, f32[9,128,128]{2,1,0:T(8,128)} %bitcast.112, f32[3,16,256]{2,1,0:T(8,128)} %get-tuple-element.114.target_ref, bf16[32,512]{1,0:T(8,128)(2,1)} %constant.106.clone.lines_ref, ...), custom_call_target="tpu_custom_call" | custom-call | tf_op jit(solution)/shard_map/render/pallas_call | solution.py:764
  171.4 1.1 copy-done
  172.4 21.7 %owner_scatter.3 = (f32[144,128]{1,0:T(8,128)S(1)}, f32[1,128]{1,0:T(1,128)S(1)}) custom-call(f32[10,2,64,128]{3,2,1,0:T(8,128)S(1)} %bitcast.110, f32[2,128,128]{2,1,0:T(8,128)S(1)} %get-tuple-element.34.shift_ref, s32[4,128,128]{2,1,0:T(8,128)S(1)} %bitcast.109), custom_call_target="tpu_custom_call" | custom-call | tf_op jit(solution)/shard_map/owner_scatter/pallas_call | solution.py:563
  194.2 0.6 maximum_multiply_fusion
  194.8 0.7 pad_maximum_fusion
  195.5 0.1 broadcast_multiply_fusion
  195.6 0.6 slice_divide_fusion.1
  196.2 0.3 slice_divide_fusion
  196.5 0.4 fusion.13
  196.9 1.3 fusion.23
  198.2 1.6 divide_subtract_fusion
  (45 shorter events, 0.3 us)
Async XLA Ops:
  0.6 0.7 copy-start.12
  2.0 0.7 copy-start.13
  4.1 2.9 %copy-start.8 = (f32[2,16,3,256]{3,1,2,0:T(8,128)S(1)}, f32[2,16,3,256]{3,1,2,0:T(8,128)}, u32[]{:S(2)}) copy-start(f32[2,16,3,256]{3,1,2,0:T(8,128)} %param.20) | copy-start | bytes 294916
  4.1 3.9 %copy-start.5 = (f32[55,2048]{1,0:T(8,128)S(1)}, f32[55,2048]{1,0:T(8,128)}, u32[]{:S(2)}) copy-start(f32[55,2048]{1,0:T(8,128)} %param.15) | copy-start | bytes 1351684
  8.1 0.8 copy-start.9
  9.1 0.8 copy-start.4
  54.3 0.8 copy-start.3
  90.1 1.1 copy-start.1
  113.2 2.8 %copy-start.7 = (f32[55,2048]{1,0:T(8,128)S(1)}, f32[55,2048]{1,0:T(8,128)}, u32[]{:S(2)}) copy-start(f32[55,2048]{1,0:T(8,128)} %param.17) | copy-start | bytes 1351684
  113.3 2.7 %copy-start.6 = (f32[55,2048]{1,0:T(8,128)S(1)}, f32[55,2048]{1,0:T(8,128)}, u32[]{:S(2)}) copy-start(f32[55,2048]{1,0:T(8,128)} %param.16) | copy-start | bytes 1351684
  135.4 0.8 copy-start.2
  171.4 1.1 copy-start
  172.4 22.4 %copy-start.10 = (f32[3,16,256]{2,1,0:T(8,128)S(1)}, f32[3,16,256]{2,1,0:T(8,128)}, u32[]{:S(2)}) copy-start(f32[3,16,256]{2,1,0:T(8,128)} %get-tuple-element.37) | copy-start | bytes 147460
  172.4 22.4 %copy-start.11 = (f32[3,16,256]{2,1,0:T(8,128)S(1)}, f32[3,16,256]{2,1,0:T(8,128)}, u32[]{:S(2)}) copy-start(f32[3,16,256]{2,1,0:T(8,128)} %get-tuple-element.38) | copy-start | bytes 147460

commit v6 on v3

--- a/solution.py
+++ b/solution.py
@@ -194,31 +194,33 @@
     )
 
 
-GROUP = 4
+GROUP = 16
 
 
 def routing_kernel(ids_ref, tile_ref, upper_ref, slot_ref, asked_ref, request, send_sem, recv_sem):
     greet()
     row_iota = lax.broadcasted_iota(I32, (OWN, LANES), 0)
     own_tile = (lax.broadcasted_iota(I32, (1, LANES), 1) & (TILES_DEV - 1)).astype(F32)
-    zero = jnp.zeros((OWN, LANES), F32)
+    zero = jnp.zeros((OWN, LANES), BF16)
     upper = upper_ref[...]
 
     def body(k, carry):
         out = []
         for s in range(STEPS):
-            counts, acc = carry[s]
+            earlier, acc = carry[s]
             members, cells = [], []
             for c in range(GROUP):
                 ids = ids_ref[s, pl.ds(k * GROUP + c, 1), :]
                 owner = lax.shift_right_logical(ids, 11)
                 member = row_iota == owner
                 member_bf = jnp.where(member, 1.0, 0.0).astype(BF16)
-                ahead = jnp.dot(member_bf, upper, preferred_element_type=F32)
+                ahead = jnp.dot(
+                    jnp.concatenate([member_bf, earlier], 1), upper, preferred_element_type=F32
+                )
                 rank = jnp.sum(
-                    jnp.where(member, ahead[:, :LANES] + counts, 0.0), axis=0, keepdims=True
+                    jnp.where(member, ahead, 0.0), axis=0, keepdims=True
                 ).astype(I32)
-                counts = counts + ahead[:, LANES:]
+                earlier = earlier + member_bf
                 slot_ref[s, pl.ds(k * GROUP + c, 1), :] = owner * LANES + rank
                 here = row_iota == rank
                 low = (ids & 127).astype(F32)
@@ -239,7 +241,7 @@
                 (((1,), (1,)), ((), ())),
                 preferred_element_type=F32,
             )
-            out.append((counts, acc))
+            out.append((earlier, acc))
         return tuple(out)
 
     start = tuple((zero, jnp.zeros((OWN, 2 * LANES), F32)) for _ in range(STEPS))
@@ -270,7 +272,7 @@
 
 def routing(ids, lane_tiles):
     strict = np.triu(np.ones((128, 128), np.float32), 1)
-    upper = jnp.asarray(np.concatenate([strict, np.ones((128, 128), np.float32)], 1), BF16)
+    upper = jnp.asarray(np.concatenate([strict, np.ones((128, 128), np.float32)], 0), BF16)
     vmem = pl.BlockSpec(memory_space=pltpu.VMEM)
     return pl.pallas_call(
         routing_kernel,

time: 199 us -> 193 us (0.970)
  Pallas kernels: 173 us -> 167 us
    pallas_call x1, Pallas kernels: 28 us -> 21.8 us  [routing(): pl.pallas_call(routing_kernel, out_shape=(jax.ShapeDtypeStruct((STEPS, SL...]
where the time goes in v6:
time: 193 us
  Pallas kernels  167 us (87%)
  other arithmetic  15.3 us (8%)
  local copies, waits for them, and re-layouts  9.65 us (5%)
    pallas_call x2, Pallas kernels, render(): pl.pallas_call(render_kernel, out_shape=(jax.ShapeDtypeStruct((3, TILES_D...  70.1 us
    pallas_call x2, Pallas kernels, owner_scatter(): pl.pallas_call(functools.partial(scatter_kernel, step), out_shape=(jax.Sh...  42.1 us
    pallas_call x2, Pallas kernels, owner_gather(): pl.pallas_call(functools.partial(gather_kernel, step), out_shape=(jax.Sha...  32.9 us
    pallas_call x1, Pallas kernels, routing(): pl.pallas_call(routing_kernel, out_shape=(jax.ShapeDtypeStruct((STEPS, SL...  21.8 us
    unnamed x38, local copies, waits for them, and re-layouts  6.7 us
    select_n x2, other arithmetic, factor_rows(): beta = jnp.where(has_a, half_log2e * conic_b / root, 0.0)  4.36 us

profile of v6, /device:TPU:1, one launch (start us, length us, event | category | flops | bytes accessed | tf_op | source)
XLA Modules:
  0.0 192.9 jit_solution(4655225383948520215)
XLA Ops:
  0.6 0.7 copy-done.12
  1.3 0.7 fusion.81
  2.0 0.7 copy-done.13
  2.7 0.1 tile.9.tile_ref
  2.7 1.3 select_multiply_fusion.1
  4.1 0.0 copy-start.8
  4.1 2.8 %multiply_select_fusion.2 = (f32[1,2048]{1,0:T(1,128)S(1)}, f32[1,2048]{1,0:T(1,128)S(1)}, f32[1,2048]{1,0:T(1,128)S(1)}, f32[1,2048]{1,0:T(1,128)S(1)}, f32[1,2...) fusion(f32[1,2048]{1,0:T(1,128)S(1)} %get-tuple-element.83, ...), kind=kLoop, calls=%fused_computation.162 | loop fusion | flops 63488 | bytes 147464 | tf_op jit(solution)/shard_map/jit(_where)/select_n | solution.py:115
  7.0 0.6 slice_bitcast_fusion
  7.6 0.1 multiply_multiply_fusion.18
  7.7 0.2 stack.12
  8.0 0.1 multiply_reduce_fusion.3
  8.1 0.8 copy-done.9
  8.9 0.2 copy.20
  9.1 0.0 copy-start.4
  9.1 0.2 reshape.208.ids_ref
  9.3 0.6 copy-done.4
  10.0 21.8 %routing.1 = (s32[2,64,128]{2,1,0:T(8,128)S(1)}, s32[4,128,128]{2,1,0:T(8,128)S(1)}) custom-call(s32[2,64,128]{2,1,0:T(8,128)S(1)} %reshape.208.ids_ref, s32[2,1,128]{2,1,0:T(1,128)S(1)} %tile.9.tile_ref, bf16[256,128]{1,0:T(8,128)(2,1)S(1)} %copy-done.4), custom_call_target="tpu_custom_call" | custom-call | tf_op jit(solution)/shard_map/routing/pallas_call | solution.py:277
  31.8 0.6 slice_bitcast_fusion.2
  32.4 16.3 %owner_gather.2 = (f32[9,128,128]{2,1,0:T(8,128)S(1)}, f32[2,128,128]{2,1,0:T(8,128)S(1)}) custom-call(f32[9,16,128]{2,1,0:T(8,128)S(1)} %constant_dynamic-update-slice_fusion.table_ref, s32[4,128,128]{2,1,0:T(8,128)S(1)} %get-tuple-element.25.asked_ref), custom_call_target="tpu_custom_call" | custom-call | tf_op jit(solution)/shard_map/owner_gather/pallas_call | solution.py:386
  48.7 0.8 copy-done.3
  49.5 35.0 %render.2 = (f32[3,16,256]{2,1,0:T(8,128)}, f32[10,128,128]{2,1,0:T(8,128)}) custom-call(s32[8192]{0:T(1024)} %get-tuple-element.127.slot_ref, f32[9,128,128]{2,1,0:T(8,128)} %copy-done.3, f32[3,16,256]{2,1,0:T(8,128)} %get-tuple-element.115.target_ref, bf16[32,512]{1,0:T(8,128)(2,1)} %constant.106.clone.lines_ref, ...), custom_call_target="tpu_custom_call" | custom-call | tf_op jit(solution)/shard_map/render/pallas_call | solution.py:704
  84.5 1.1 copy-done.1
  85.6 21.1 %owner_scatter.2 = (f32[144,128]{1,0:T(8,128)S(1)}, f32[1,128]{1,0:T(1,128)S(1)}) custom-call(f32[10,128,128]{2,1,0:T(8,128)S(1)} %copy-done.1, f32[2,128,128]{2,1,0:T(8,128)S(1)} %get-tuple-element.28.shift_ref, s32[4,128,128]{2,1,0:T(8,128)S(1)} %get-tuple-element.25.asked_ref), custom_call_target="tpu_custom_call" | custom-call | tf_op jit(solution)/shard_map/owner_scatter/pallas_call | solution.py:505
  106.7 0.0 copy-start.7
  106.8 0.1 broadcast_multiply_fusion.1
  106.8 0.6 slice_divide_fusion.3
  107.5 0.3 slice_divide_fusion.2
  107.8 0.4 fusion.2
  108.1 1.4 fusion.12
  109.6 0.5 divide_subtract_fusion.1
  110.0 0.3 select_multiply_fusion
  110.4 1.6 multiply_select_fusion
  112.1 0.1 multiply_multiply_fusion.9
  112.2 0.2 stack.13
  112.4 0.1 multiply_reduce_fusion.1
  112.5 16.6 %owner_gather.3 = (f32[9,128,128]{2,1,0:T(8,128)S(1)}, f32[2,128,128]{2,1,0:T(8,128)S(1)}) custom-call(f32[9,16,128]{2,1,0:T(8,128)S(1)} %constant_dynamic-update-slice_fusion.7.table_ref, s32[4,128,128]{2,1,0:T(8,128)S(1)} %get-tuple-element.25.asked_ref), custom_call_target="tpu_custom_call" | custom-call | tf_op jit(solution)/shard_map/owner_gather/pallas_call | solution.py:386
  129.2 0.8 copy-done.2
  130.0 35.1 %render.3 = (f32[3,16,256]{2,1,0:T(8,128)}, f32[10,128,128]{2,1,0:T(8,128)}) custom-call(s32[8192]{0:T(1024)} %get-tuple-element.126.slot_ref, f32[9,128,128]{2,1,0:T(8,128)} %copy-done.2, f32[3,16,256]{2,1,0:T(8,128)} %get-tuple-element.114.target_ref, bf16[32,512]{1,0:T(8,128)(2,1)} %constant.106.clone.lines_ref, ...), custom_call_target="tpu_custom_call" | custom-call | tf_op jit(solution)/shard_map/render/pallas_call | solution.py:704
  165.2 1.1 copy-done
  166.2 21.0 %owner_scatter.3 = (f32[144,128]{1,0:T(8,128)S(1)}, f32[1,128]{1,0:T(1,128)S(1)}) custom-call(f32[10,128,128]{2,1,0:T(8,128)S(1)} %copy-done, f32[2,128,128]{2,1,0:T(8,128)S(1)} %get-tuple-element.34.shift_ref, s32[4,128,128]{2,1,0:T(8,128)S(1)} %get-tuple-element.25.asked_ref), custom_call_target="tpu_custom_call" | custom-call | tf_op jit(solution)/shard_map/owner_scatter/pallas_call | solution.py:505
  187.3 0.6 maximum_multiply_fusion
  187.9 0.7 pad_maximum_fusion
  188.6 0.1 broadcast_multiply_fusion
  188.7 0.6 slice_divide_fusion.1
  189.3 0.3 slice_divide_fusion
  189.6 0.4 fusion.13
  189.9 1.3 fusion.23
  191.3 1.6 divide_subtract_fusion
  (45 shorter events, 0.3 us)
Async XLA Ops:
  0.6 0.7 copy-start.12
  2.0 0.7 copy-start.13
  4.1 2.9 %copy-start.8 = (f32[2,16,3,256]{3,1,2,0:T(8,128)S(1)}, f32[2,16,3,256]{3,1,2,0:T(8,128)}, u32[]{:S(2)}) copy-start(f32[2,16,3,256]{3,1,2,0:T(8,128)} %param.20) | copy-start | bytes 294916
  4.1 3.9 %copy-start.5 = (f32[55,2048]{1,0:T(8,128)S(1)}, f32[55,2048]{1,0:T(8,128)}, u32[]{:S(2)}) copy-start(f32[55,2048]{1,0:T(8,128)} %param.15) | copy-start | bytes 1351684
  8.1 0.8 copy-start.9
  9.1 0.8 copy-start.4
  48.7 0.8 copy-start.3
  84.5 1.1 copy-start.1
  106.7 2.8 %copy-start.7 = (f32[55,2048]{1,0:T(8,128)S(1)}, f32[55,2048]{1,0:T(8,128)}, u32[]{:S(2)}) copy-start(f32[55,2048]{1,0:T(8,128)} %param.17) | copy-start | bytes 1351684
  106.8 2.7 %copy-start.6 = (f32[55,2048]{1,0:T(8,128)S(1)}, f32[55,2048]{1,0:T(8,128)}, u32[]{:S(2)}) copy-start(f32[55,2048]{1,0:T(8,128)} %param.16) | copy-start | bytes 1351684
  129.2 0.8 copy-start.2
  165.2 1.1 copy-start
  166.2 21.7 %copy-start.10 = (f32[3,16,256]{2,1,0:T(8,128)S(1)}, f32[3,16,256]{2,1,0:T(8,128)}, u32[]{:S(2)}) copy-start(f32[3,16,256]{2,1,0:T(8,128)} %get-tuple-element.37) | copy-start | bytes 147460
  166.2 21.7 %copy-start.11 = (f32[3,16,256]{2,1,0:T(8,128)S(1)}, f32[3,16,256]{2,1,0:T(8,128)}, u32[]{:S(2)}) copy-start(f32[3,16,256]{2,1,0:T(8,128)} %get-tuple-element.38) | copy-start | bytes 147460
